TPU v7x, 512 devices: a whole 4x8x8 slice. The times are simulated.
512 devices in a mesh: dp: 8 (over y), tp: 64 (over z, x, core).
Axes of the slice: x: 4, y: 8, z: 8, core: 2. Of those that a mesh axis runs over, the one named last changes fastest.
Arguments:
- tokens: bfloat16 [32768, 2048], P(('dp', 'tp')), parts along dimension 0, may hold values from -6 to 6
- norm_gain: float32 [2048], replicated, may hold values from 0.1 to 1.9
- routes: int32 [32768, 8], P(('dp', 'tp')), parts along dimension 0, may hold values from 0 to 31, all different within a row; in each aligned block of 64 rows (0 to 63, 64 to 127, ...) at most 24 rows name the same one
- gate_codes: int32 [32768, 8], P(('dp', 'tp')), parts along dimension 0, may hold values from 1 to 8191
- gate_weight: bfloat16 [64, 2048, 384], P('tp'), may hold values from -0.125 to 0.125
- up_weight: bfloat16 [64, 2048, 384], P('tp'), may hold values from -0.125 to 0.125
- down_weight: bfloat16 [64, 384, 2048], P('tp'), may hold values from -0.21875 to 0.21875
Outputs:
- mixed: bfloat16 [32768, 2048], P(('dp', 'tp')), parts along dimension 0
There are 8 independent parts, one for each index of `dp`. A program takes and returns all parts, laid end to end along the dimension named above; an argument that names none is the same for every part. Nothing has to cross between parts.
Inputs may be any that keep to these rules, and one draw needn't show every extreme that they name: `routes`: each row names 8 different experts; among the 64 rows of one device no expert is named more than 24 times, and some device names some expert exactly 24 times.
All inputs are finite; a program needn't handle non-finite values.
Results may differ from a plain program's by a relative error of at most 0.0071.
Values may be sent and summed in bfloat16 or wider, within the bound.
No kernel may reach another device: no remote copies, remote signals or barrier semaphores. Data moves between devices by JAX's collectives and lax.ppermute only.
A program may use at most 128 MiB of HBM per device.

v0:
```python
import jax
import jax.numpy as jnp
from jax import lax
from jax.sharding import PartitionSpec as P


def swapped(x, axis, apart):
    return lax.ppermute(x, axis, [(i, i ^ 1 << apart) for i in range(lax.axis_size(axis))])


def expert_slice(arrived, gate_part, up_part, down_part):
    gate_value = jnp.einsum("sid,dh->sih", arrived, gate_part, preferred_element_type=jnp.float32)
    up_value = jnp.einsum("sid,dh->sih", arrived, up_part, preferred_element_type=jnp.float32)
    hidden = (jax.nn.silu(gate_value) * up_value).astype(jnp.bfloat16)
    return jnp.einsum("sih,hd->sid", hidden, down_part, preferred_element_type=jnp.float32)


def local(tokens, norm_gain, routes, gate_codes, gate_weight, up_weight, down_weight):
    row_count, feature_count = tokens.shape
    route_count = routes.shape[1]
    devices = lax.axis_size("tp")
    experts = devices // 2
    own_half = lax.axis_index("tp") % 2
    capacity = 2 * min(row_count // 2, row_count * route_count * 3 // (experts * 4))
    half_capacity = capacity // 2
    widened = tokens.astype(jnp.float32)
    scale_rows = lax.rsqrt(jnp.mean(widened * widened, axis=1, keepdims=True) + 1e-06)
    normed = (widened * scale_rows * norm_gain[None, :]).astype(jnp.bfloat16)
    gate_scale = gate_codes.astype(jnp.float32) / 32768.0
    flat_expert = routes.reshape(-1)
    one_hot = (flat_expert[:, None] == jnp.arange(experts, dtype=jnp.int32)[None, :]).astype(
        jnp.int32
    )
    earlier = jnp.cumsum(one_hot, axis=0) - one_hot
    position = jnp.sum(earlier * one_hot, axis=1)
    slot_index = flat_expert * capacity + position
    source_row = jnp.arange(row_count * route_count, dtype=jnp.int32) // route_count
    outgoing = (
        jnp.zeros((experts * capacity, feature_count), jnp.bfloat16)
        .at[slot_index]
        .set(normed[source_row])
    )
    outgoing = outgoing.reshape(experts, capacity, feature_count)
    gate_part = gate_weight[0]
    up_part = up_weight[0]
    down_part = down_weight[0]
    doubled = jnp.repeat(outgoing, 2, axis=0)
    partial_value = expert_slice(
        lax.all_to_all(doubled, "tp", split_axis=0, concat_axis=0, tiled=True),
        gate_part,
        up_part,
        down_part,
    )
    lower_half = partial_value[:, :half_capacity]
    upper_half = partial_value[:, half_capacity:]
    own_part = jnp.where(own_half == 0, lower_half, upper_half)
    given_part = jnp.where(own_half == 0, upper_half, lower_half)
    received = swapped(given_part, "tp", 0)
    finished = (own_part + received).astype(jnp.bfloat16)
    returned = lax.all_to_all(finished, "tp", split_axis=0, concat_axis=0, tiled=True)
    flat_out = returned.reshape(experts * capacity, feature_count)
    picked = flat_out[slot_index].reshape(row_count, route_count, feature_count).astype(jnp.float32)
    return jnp.sum(gate_scale[:, :, None] * picked, axis=1).astype(jnp.bfloat16)


def solution(mesh):
    placed = (
        P(("dp", "tp"), None),
        P(),
        P(("dp", "tp"), None),
        P(("dp", "tp"), None),
        P("tp", None, None),
        P("tp", None, None),
        P("tp", None, None),
    )
    return jax.shard_map(
        local, mesh=mesh, in_specs=placed, out_specs=P(("dp", "tp"), None), check_vma=False
    )
```

profile of v0, /device:TPU:56, one launch (start us, length us, event | category | flops | bytes accessed | tf_op | source)
XLA Modules:
  0.0 359.6 jit_solution(17274776548023467477)
XLA Ops:
  0.0 0.0 copy-start
  0.0 0.9 copy.16
  0.9 0.1 eq.36
  1.0 0.1 eq.32
  1.1 0.7 broadcast_multiply_fusion
  1.8 1.2 reduce-window.6
  3.0 0.2 slice_reduce_fusion
  3.2 0.1 copy.15
  3.3 0.1 mul.56
  3.4 1.1 fusion.13
  4.5 0.1 fusion.18
  4.7 1.1 fusion.15
  5.7 12.3 %scatter_custom_fusion = bf16[768,2048]{1,0:T(8,128)(2,1)} fusion(s32[512]{0:T(512)S(1)} %bitcast.45, bf16[64,2048]{1,0:T(8,128)(2,1)S(1)} %fusion.15, s32[1024]{0:T(1024)S(1)} %pad_clamp_fusion.1, bf16[]{:T(256)} %constant.49.clone.1), kind=kCustom, calls=%fused_computation.9 | custom fusion | bytes 3145730 | tf_op jit(solution)/shard_map/scatter | solution.py:41
  18.1 5.5 %broadcast_in_dim.5 = bf16[32,2,24,2048]{3,2,1,0:T(8,128)(2,1)} broadcast(bf16[32,24,2048]{2,1,0:T(8,128)(2,1)} %bitcast.44), dimensions={0,2,3} | broadcast | bytes 9437184 | tf_op jit(solution)/shard_map/broadcast_in_dim | solution.py:47
  23.6 0.0 copy-start.4
  23.6 14.1 %all-to-all-start = ((bf16[64,24,2048]{2,1,0:T(8,128)(2,1)}), bf16[64,24,2048]{2,1,0:T(8,128)(2,1)}, u32[]{:S(2)}, u32[]{:S(2)}) async-start(bf16[64,24,2048]{2,1,0:T(8,128)(2,1)} %bitcast.43), calls=%async_computation | async-start | bytes 12582912 | tf_op jit(solution)/shard_map/all_to_all | solution.py:49
  37.8 141.2 %all-to-all-done = bf16[64,24,2048]{2,1,0:T(8,128)(2,1)} async-done(((bf16[64,24,2048]{2,1,0:T(8,128)(2,1)}), bf16[64,24,2048]{2,1,0:T(8,128)(2,1)}, u32[]{:S(2)}, u32[]{:S(2)}) %all-to-all-start) | async-done | bytes 6291488 | tf_op jit(solution)/shard_map/all_to_all | solution.py:49
  178.9 0.0 copy-done.4
  178.9 7.7 %fusion.6 = f32[64,24,384]{2,1,0:T(8,128)} fusion(bf16[64,24,2048]{2,1,0:T(8,128)(2,1)} %all-to-all-done, bf16[1,2048,384]{2,1,0:T(8,128)(2,1)S(1)} %copy-done.4), kind=kOutput, calls=%fused_computation.13 | convolution fusion | flops 2415919104 | bytes 10223616 | tf_op jit(solution)/shard_map/sid,dh->sih/dot_general | solution.py:13
  186.6 0.0 copy-done
  186.6 12.4 %fusion.4 = f32[64,24,2048]{2,1,0:T(8,128)} fusion(bf16[1,384,2048]{2,1,0:T(8,128)(2,1)S(1)} %copy-done, f32[64,24,384]{2,1,0:T(8,128)} %fusion.6, bf16[64,24,2048]{2,1,0:T(8,128)(2,1)} %all-to-all-done, bf16[1,2048,384]{2,1,0:T(8,128)(2,1)} %param.11), kind=kOutput, calls=%fused_computation.11 | convolution fusion | flops 4835377152 | bytes 24379392 | tf_op jit(solution)/shard_map/sih,hd->sid/dot_general | solution.py:15
  199.0 11.9 %slice_select_fusion = f32[64,12,2048]{2,1,0:T(8,128)} fusion(f32[64,24,2048]{2,1,0:T(8,128)} %fusion.4, pred[]{:T(512)S(6)} %eq.31), kind=kLoop, calls=%fused_computation.5 | loop fusion | flops 1572864 | bytes 18874368 | tf_op jit(solution)/shard_map/jit(_where)/select_n | solution.py:57
  210.9 0.0 copy-start.2
  210.9 7.2 %copy.19 = f32[64,12,2048]{2,0,1:T(8,128)S(1)} copy(f32[64,12,2048]{2,1,0:T(8,128)} %slice_select_fusion) | data formatting | bytes 12582912 | tf_op jit(solution)/shard_map/jit(_where)/select_n | solution.py:57
  218.1 2.1 collective-permute-start
  220.2 10.0 %collective-permute-done = f32[64,12,2048]{2,0,1:T(8,128)} collective-permute-done((f32[64,12,2048]{2,0,1:T(8,128)S(1)}, f32[64,12,2048]{2,0,1:T(8,128)}, u32[]{:S(2)}, u32[]{:S(2)}) %collective-permute-start) | collective-permute-done | bytes 6291488 | tf_op jit(solution)/shard_map/ppermute | solution.py:8
  230.3 0.0 copy-done.2
  230.3 9.1 %fusion = bf16[64,12,2048]{2,1,0:T(8,128)(2,1)} fusion(f32[64,12,2048]{2,0,1:T(8,128)} %collective-permute-done, f32[64,24,2048]{2,1,0:T(8,128)S(1)} %copy-done.2, pred[]{:T(512)S(6)} %eq.31), kind=kLoop, calls=%fused_computation.4 | loop fusion | flops 4718592 | bytes 22020096 | tf_op jit(solution)/shard_map/convert_element_type | solution.py:59
  239.3 0.0 copy-start.3
  239.3 6.0 %all-to-all-start.1 = ((bf16[64,12,2048]{2,1,0:T(8,128)(2,1)}), bf16[64,12,2048]{2,1,0:T(8,128)(2,1)}, u32[]{:S(2)}, u32[]{:S(2)}) async-start(bf16[64,12,2048]{2,1,0:T(8,128)(2,1)} %fusion), calls=%async_computation.1 | async-start | bytes 8388608 | tf_op jit(solution)/shard_map/all_to_all | solution.py:60
  245.3 0.0 copy-done.3
  245.4 0.1 copy.14
  245.5 96.1 %all-to-all-done.1 = bf16[64,12,2048]{2,1,0:T(8,128)(2,1)} async-done(((bf16[64,12,2048]{2,1,0:T(8,128)(2,1)}), bf16[64,12,2048]{2,1,0:T(8,128)(2,1)}, u32[]{:S(2)}, u32[]{:S(2)}) %all-to-all-start.1) | async-done | bytes 3145760 | tf_op jit(solution)/shard_map/all_to_all | solution.py:60
  341.6 6.2 %reshape.114 = bf16[768,2048]{1,0:T(8,128)(2,1)} reshape(bf16[64,12,2048]{2,1,0:T(8,128)(2,1)} %all-to-all-done.1) | data formatting | bytes 6291456 | tf_op jit(solution)/shard_map/reshape | solution.py:61
  347.7 0.0 copy-start.1
  347.7 7.7 %gather_fusion = bf16[512,2048]{1,0:T(8,128)(2,1)} fusion(bf16[768,2048]{1,0:T(8,128)(2,1)} %reshape.114, s32[1024]{0:T(1024)S(1)} %pad_clamp_fusion), kind=kCustom, calls=%fused_computation.1 | custom fusion | bytes 4196352 | tf_op jit(solution)/shard_map/gather | solution.py:62
  355.4 4.1 %fusion.1 = bf16[64,2048]{1,0:T(8,128)(2,1)} fusion(bf16[512,2048]{1,0:T(8,128)(2,1)} %gather_fusion, f32[64,8]{1,0:T(8,128)S(1)} %copy.14), kind=kLoop, calls=%fused_computation.7 | loop fusion | flops 3014656 | bytes 2361344 | tf_op jit(solution)/shard_map/reduce_sum | solution.py:63
  359.6 0.0 copy-done.1
  (9 shorter events, 0.1 us)
Async XLA Ops:
  0.0 186.6 %copy-start = (bf16[1,384,2048]{2,1,0:T(8,128)(2,1)S(1)}, bf16[1,384,2048]{2,1,0:T(8,128)(2,1)}, u32[]{:S(2)}) copy-start(bf16[1,384,2048]{2,1,0:T(8,128)(2,1)} %param.13) | copy-start | bytes 4718596
  23.6 155.3 %copy-start.4 = (bf16[1,2048,384]{2,1,0:T(8,128)(2,1)S(1)}, bf16[1,2048,384]{2,1,0:T(8,128)(2,1)}, u32[]{:S(2)}) copy-start(bf16[1,2048,384]{2,1,0:T(8,128)(2,1)} %param.12) | copy-start | bytes 4718596
  23.6 155.3 %all-to-all-start = ((bf16[64,24,2048]{2,1,0:T(8,128)(2,1)}), bf16[64,24,2048]{2,1,0:T(8,128)(2,1)}, u32[]{:S(2)}, u32[]{:S(2)}) async-start(bf16[64,24,2048]{2,1,0:T(8,128)(2,1)} %bitcast.43), calls=%async_computation | async-start | bytes 12582912 | tf_op jit(solution)/shard_map/all_to_all | solution.py:49
  210.9 19.4 %copy-start.2 = (f32[64,24,2048]{2,1,0:T(8,128)S(1)}, f32[64,24,2048]{2,1,0:T(8,128)}, u32[]{:S(2)}) copy-start(f32[64,24,2048]{2,1,0:T(8,128)} %fusion.4) | copy-start | bytes 37748740
  218.1 12.2 %collective-permute-start = (f32[64,12,2048]{2,0,1:T(8,128)S(1)}, f32[64,12,2048]{2,0,1:T(8,128)}, u32[]{:S(2)}, u32[]{:S(2)}) collective-permute-start(f32[64,12,2048]{2,0,1:T(8,128)S(1)} %copy.19), channel_id=1, source_target_pairs={{0,1},{1,0},{2,3},{3,2},{4,5},{5,4},{6,7},{7,6},{8,9},{9,8},{10,11... | collective-permute-start | bytes 18874376 | tf_op jit(solution)/shard_map/ppermute | solution.py:8
  239.3 6.0 %copy-start.3 = (s32[64,8]{0,1:T(8,128)S(1)}, s32[64,8]{0,1:T(8,128)}, u32[]{:S(2)}) copy-start(s32[64,8]{0,1:T(8,128)} %param.10) | copy-start | bytes 6148
  239.3 102.2 %all-to-all-start.1 = ((bf16[64,12,2048]{2,1,0:T(8,128)(2,1)}), bf16[64,12,2048]{2,1,0:T(8,128)(2,1)}, u32[]{:S(2)}, u32[]{:S(2)}) async-start(bf16[64,12,2048]{2,1,0:T(8,128)(2,1)} %fusion), calls=%async_computation.1 | async-start | bytes 8388608 | tf_op jit(solution)/shard_map/all_to_all | solution.py:60
  347.7 11.8 %copy-start.1 = (bf16[1,384,2048]{2,1,0:T(8,128)(2,1)S(1)}, bf16[1,384,2048]{2,1,0:T(8,128)(2,1)}, u32[]{:S(2)}) copy-start(bf16[1,384,2048]{2,1,0:T(8,128)(2,1)} %param.13) | copy-start | bytes 4718596
where the time goes:
time: 360 us
  waiting for transfers between devices  247 us (69%)
  local copies, waits for them, and re-layouts  40.4 us (11%)
  other arithmetic  29.4 us (8%)
  starting transfers between devices  22.3 us (6%)
  matrix products  20 us (6%)
    all_to_all x1, waiting for transfers between devices, local(): lax.all_to_all(doubled, 'tp', split_axis=0, concat_axis=0, tiled=True)  141 us
    all_to_all x1, waiting for transfers between devices, local(): lax.all_to_all(finished, 'tp', split_axis=0, concat_axis=0, tiled=True)  96.1 us
    all_to_all x1, starting transfers between devices, local(): lax.all_to_all(doubled, 'tp', split_axis=0, concat_axis=0, tiled=True)  14.1 us
    dot_general x1, matrix products, expert_slice(): jnp.einsum('sih,hd->sid', hidden, down_part, preferred_element_type=jnp.f...  12.4 us
    scatter x1, local copies, waits for them, and re-layouts, local(): outgoing = jnp.zeros((experts * capacity, feature_count), jnp.bfloat16).a...  12.3 us
    select_n x1, other arithmetic, local(): given_part = jnp.where(own_half == 0, upper_half, lower_half)  11.9 us
    ppermute x1, waiting for transfers between devices, swapped(): lax.ppermute(x, axis, [(i, i ^ 1 << apart) for i in range(lax.axis_size(a...  10 us
    convert_element_type x1, other arithmetic, local(): finished = (own_part + received).astype(jnp.bfloat16)  9.08 us
  transfers between devices with their start and end apart: 3, of which 3 were waited for; matrix products, arithmetic and copies ran while one was open for 0% of the time, Pallas kernels for 0%

commit v1 on v0

v1 whole, which is shorter than its diff:
```python
import jax
import jax.numpy as jnp
from jax import lax
from jax.experimental import pallas as pl
from jax.experimental.pallas import tpu as pltpu
from jax.sharding import Mesh, PartitionSpec as P

F32 = jnp.float32
BF16 = jnp.bfloat16
EXPERTS = 32
ROOM = 24
SLOTS = EXPERTS * ROOM


def dot(a, b, dims=((1,), (0,))):
    return lax.dot_general(a, b, (dims, ((), ())), preferred_element_type=F32)


def slot_tables(routes, rows):
    expert = lax.broadcasted_iota(jnp.int32, (rows, EXPERTS), 1)
    named = [routes[:, k : k + 1] == expert for k in range(routes.shape[1])]
    mask = sum(n.astype(F32) for n in named)
    earlier = (
        lax.broadcasted_iota(jnp.int32, (rows, rows), 1)
        < lax.broadcasted_iota(jnp.int32, (rows, rows), 0)
    ).astype(BF16)
    rank = dot(earlier, mask.astype(BF16))
    key = jnp.where(mask > 0.5, rank, -1.0)
    slot = lax.broadcasted_iota(jnp.int32, (EXPERTS, SLOTS), 1)
    owner = lax.broadcasted_iota(jnp.int32, (EXPERTS, SLOTS), 0)
    quotient = (slot * 2731) >> 16
    spread = (quotient == owner).astype(BF16)
    row_slot = lax.broadcasted_iota(jnp.int32, (rows, SLOTS), 1)
    place = (row_slot - ((row_slot * 2731) >> 16) * ROOM).astype(F32)
    chosen = dot(key.astype(BF16), spread) == place
    return named, spread, chosen


def pack_kernel(tokens_ref, gain_ref, routes_ref, out_ref):
    rows = tokens_ref.shape[0]
    widened = tokens_ref[...].astype(F32)
    scale = lax.rsqrt(jnp.mean(widened * widened, axis=1, keepdims=True) + 1e-06)
    normed = (widened * scale * gain_ref[...]).astype(BF16)
    _, _, chosen = slot_tables(routes_ref[...], rows)
    out_ref[...] = dot(chosen.astype(BF16), normed, ((0,), (0,))).astype(BF16)


def mix_kernel(picked_ref, routes_ref, codes_ref, out_ref):
    rows = routes_ref.shape[0]
    named, spread, chosen = slot_tables(routes_ref[...], rows)
    codes = codes_ref[...]
    high = codes >> 6
    low = codes - (high << 6)

    def table(part):
        by_expert = sum(
            jnp.where(n, part[:, k : k + 1].astype(F32), 0.0) for k, n in enumerate(named)
        )
        return jnp.where(chosen, dot(by_expert.astype(BF16), spread), 0.0).astype(BF16)

    picked = picked_ref[...]
    total = dot(table(high), picked) * 64.0 + dot(table(low), picked)
    out_ref[...] = (total * (1.0 / 32768.0)).astype(BF16)


def swapped(x):
    return lax.ppermute(x, "core", [(0, 1), (1, 0)])


def local(tokens, norm_gain, routes, gate_codes, gate_weight, up_weight, down_weight):
    rows, features = tokens.shape
    gates = [gate_weight[0]]
    ups = [up_weight[0]]
    downs = [down_weight[0]]
    gates.append(swapped(gates[0]))
    ups.append(swapped(ups[0]))
    downs.append(swapped(downs[0]))
    outgoing = pl.pallas_call(
        pack_kernel,
        out_shape=jax.ShapeDtypeStruct((SLOTS, features), BF16),
        name="pack",
    )(tokens, norm_gain.reshape(1, features), routes)
    arrived = lax.all_to_all(outgoing, ("z", "x"), split_axis=0, concat_axis=0, tiled=True)
    total = 0.0
    for gate, up, down in zip(gates, ups, downs):
        hidden = (jax.nn.silu(dot(arrived, gate)) * dot(arrived, up)).astype(BF16)
        total = total + dot(hidden, down)
    returned = lax.all_to_all(
        total.astype(BF16), ("z", "x"), split_axis=0, concat_axis=0, tiled=True
    )
    return pl.pallas_call(
        mix_kernel,
        out_shape=jax.ShapeDtypeStruct((rows, features), BF16),
        name="mix",
    )(returned, routes, gate_codes)


def solution(mesh):
    groups = mesh.devices.shape[0]
    chips = mesh.devices.shape[1] // 2
    wide = 4
    split = Mesh(
        mesh.devices.reshape(groups, chips // wide, wide, 2), ("dp", "z", "x", "core")
    )
    tp = ("z", "x", "core")
    placed = (
        P(("dp",) + tp, None),
        P(),
        P(("dp",) + tp, None),
        P(("dp",) + tp, None),
        P(tp, None, None),
        P(tp, None, None),
        P(tp, None, None),
    )
    return jax.shard_map(
        local, mesh=split, in_specs=placed, out_specs=P(("dp",) + tp, None), check_vma=False
    )
```

time: 360 us -> 202 us (0.56)
  waiting for transfers between devices: 247 us -> 137 us
  local copies, waits for them, and re-layouts: 40.4 us -> 3.72 us
  other arithmetic: 29.4 us -> 0 us
  Pallas kernels: 0 us -> 8.38 us
  matrix products: 20 us -> 26.1 us
    all_to_all x2, waiting for transfers between devices: 237 us -> 137 us  [the longest x1 71.2 us: local(): lax.all_to_all(total.astype(BF16), ('z', 'x'), split_axis=0, concat_axis=...]
    scatter x1 -> x0, local copies, waits for them, and re-layouts: 12.3 us -> none  [local(): outgoing = jnp.zeros((experts * capacity, feature_count), jnp.bfloat16).a...]
    select_n x3 -> x0, other arithmetic: 11.9 us -> none  [the longest x1 11.9 us: local(): given_part = jnp.where(own_half == 0, upper_half, lower_half)]
    convert_element_type x3 -> x0, other arithmetic: 10.2 us -> none  [the longest x1 9.08 us: local(): finished = (own_part + received).astype(jnp.bfloat16)]
    ppermute x1 -> x3, waiting for transfers between devices: 10 us -> 0.01 us  [swapped(): return lax.ppermute(x, 'core', [(0, 1), (1, 0)])]
    pallas_call x0 -> x2, Pallas kernels: none -> 8.38 us  [the longest x1 4.34 us: local(): pl.pallas_call(mix_kernel, out_shape=jax.ShapeDtypeStruct((rows, features...]
    gather x1 -> x0, local copies, waits for them, and re-layouts: 7.7 us -> none  [local(): flat_out[slot_index].reshape(row_count, route_count, feature_count)]
    select_n x1 -> x0, local copies, waits for them, and re-layouts: 7.17 us -> none  [local(): given_part = jnp.where(own_half == 0, upper_half, lower_half)]
  transfers between devices with their start and end apart: 3 -> 5, of which waited for: 3 -> 2; matrix products, arithmetic and copies ran while one was open for 0% -> 9% of each run, Pallas kernels for 0% -> 0%
where the time goes in v1:
time: 202 us; the launch traced here: 201 us
  waiting for transfers between devices  137 us (68%)
  matrix products  26.1 us (13%)
  starting transfers between devices  25.8 us (13%)
  Pallas kernels  8.38 us (4%)
  local copies, waits for them, and re-layouts  3.72 us (2%)
    all_to_all x1, waiting for transfers between devices, local(): lax.all_to_all(total.astype(BF16), ('z', 'x'), split_axis=0, concat_axis=...  71.2 us
    all_to_all x1, waiting for transfers between devices, local(): lax.all_to_all(outgoing, ('z', 'x'), split_axis=0, concat_axis=0, tiled=T...  66 us
    dot_general x4, matrix products, dot(): return lax.dot_general(a, b, (dims, ((), ())), preferred_element_type=F32)  26.1 us
    all_to_all x1, starting transfers between devices, local(): lax.all_to_all(outgoing, ('z', 'x'), split_axis=0, concat_axis=0, tiled=T...  13.2 us
    all_to_all x1, starting transfers between devices, local(): lax.all_to_all(total.astype(BF16), ('z', 'x'), split_axis=0, concat_axis=...  6.42 us
    ppermute x3, starting transfers between devices, swapped(): return lax.ppermute(x, 'core', [(0, 1), (1, 0)])  6.26 us
    pallas_call x1, Pallas kernels, local(): pl.pallas_call(mix_kernel, out_shape=jax.ShapeDtypeStruct((rows, features...  4.34 us
  transfers between devices with their start and end apart: 5, of which 2 were waited for; matrix products, arithmetic and copies ran while one was open for 9% of the time, Pallas kernels for 0%

profile of v1, /device:TPU:56, one launch (start us, length us, event | category | flops | bytes accessed | tf_op | source)
XLA Modules:
  0.0 201.3 jit_solution(15605967516920825970)
XLA Ops:
  0.0 1.4 copy.8.routes_ref
  1.4 4.0 %pack.1 = bf16[768,2048]{1,0:T(8,128)(2,1)} custom-call(bf16[64,2048]{1,0:T(8,128)(2,1)} %tokens_ref.1, f32[1,2048]{1,0:T(1,128)} %bitcast.29, s32[64,8]{1,0:T(8,128)} %copy.8.routes_ref), custom_call_target="tpu_custom_call" | custom-call | tf_op jit(solution)/shard_map/pack/pallas_call | solution.py:78
  5.4 13.2 %all-to-all-start = ((bf16[32,24,2048]{2,1,0:T(8,128)(2,1)}), bf16[32,24,2048]{2,1,0:T(8,128)(2,1)S(1)}, u32[]{:S(2)}, u32[]{:S(2)}) async-start(bf16[32,24,2048]{2,1,0:T(8,128)(2,1)} %bitcast.22), calls=%async_computation | async-start | bytes 6291456 | tf_op jit(solution)/shard_map/all_to_all | solution.py:83
  18.6 1.9 collective-permute-start
  20.5 2.4 %collective-permute-start.1 = (bf16[2048,384]{1,0:T(8,128)(2,1)}, bf16[2048,384]{1,0:T(8,128)(2,1)}, u32[]{:S(2)}, u32[]{:S(2)}) collective-permute-start(bf16[2048,384]{1,0:T(8,128)(2,1)} %bitcast.31), channel_id=1, source_target_pairs={{0,1},{1,0},{2,3},{3,2},{4,5},{5,4},{6,7},{7,6},{8,9},{9,8},{10,11... | collective-permute-start | bytes 4718600 | tf_op jit(solution)/shard_map/ppermute | solution.py:67
  22.9 1.9 collective-permute-start.2
  24.9 66.0 %all-to-all-done = bf16[32,24,2048]{2,1,0:T(8,128)(2,1)S(1)} async-done(((bf16[32,24,2048]{2,1,0:T(8,128)(2,1)}), bf16[32,24,2048]{2,1,0:T(8,128)(2,1)S(1)}, u32[]{:S(2)}, u32[]{:S(2)}) %all-to-all-start) | async-done | bytes 3145760 | tf_op jit(solution)/shard_map/all_to_all | solution.py:83
  90.9 4.2 %fusion.12 = f32[768,384]{1,0:T(8,128)} fusion(bf16[768,2048]{1,0:T(8,128)(2,1)S(1)} %bitcast.24, bf16[1,2048,384]{2,1,0:T(8,128)(2,1)} %param.11), kind=kOutput, calls=%fused_computation.14 | convolution fusion | flops 1207959552 | bytes 5898240 | tf_op jit(solution)/shard_map/dot_general | solution.py:16
  95.1 0.0 collective-permute-done
  95.1 4.3 %fusion.18 = f32[768,384]{1,0:T(8,128)} fusion(bf16[768,2048]{1,0:T(8,128)(2,1)S(1)} %bitcast.25, bf16[2048,384]{1,0:T(8,128)(2,1)} %collective-permute-done), kind=kOutput, calls=%fused_computation.19 | convolution fusion | flops 1207959552 | bytes 5898240 | tf_op jit(solution)/shard_map/dot_general | solution.py:16
  99.4 8.3 %fusion.1 = f32[768,2048]{1,0:T(8,128)} fusion(bf16[768,2048]{1,0:T(8,128)(2,1)S(1)} %bitcast.26, f32[768,384]{1,0:T(8,128)} %fusion.12, bf16[1,384,2048]{2,1,0:T(8,128)(2,1)} %param.13, bf16[1,2048,384]{2,1,0:T(8,128)(2,1)} %param.12), kind=kOutput, calls=%fused_computation.3 | convolution fusion | flops 2417688576 | bytes 13762560 | tf_op jit(solution)/shard_map/dot_general | solution.py:16
  107.7 0.0 collective-permute-done.1
  107.7 0.0 collective-permute-done.2
  107.7 9.2 %add_convert_fusion = bf16[768,2048]{1,0:T(8,128)(2,1)} fusion(f32[768,2048]{1,0:T(8,128)} %fusion.1, bf16[384,2048]{1,0:T(8,128)(2,1)} %collective-permute-done.2, f32[768,384]{1,0:T(8,128)} %fusion.18, bf16[768,2048]{1,0:T(8,128)(2,1)S(1)} %bitcast.27, bf16[2048,384]{1,0:T(8,128)(2,1)} %collective-permute-done.1), kind=kOutput, calls=%fused_computation | convolution fusion | flops 2420834304 | bytes 16908288 | tf_op jit(solution)/shard_map/dot_general | solution.py:16
  117.0 0.0 copy-start.1
  117.0 6.4 %all-to-all-start.1 = ((bf16[32,24,2048]{2,1,0:T(8,128)(2,1)}), bf16[32,24,2048]{2,1,0:T(8,128)(2,1)S(1)}, u32[]{:S(2)}, u32[]{:S(2)}) async-start(bf16[32,24,2048]{2,1,0:T(8,128)(2,1)} %bitcast.28), calls=%async_computation.1 | async-start | bytes 6291456 | tf_op jit(solution)/shard_map/all_to_all | solution.py:88
  123.4 0.0 copy-done.1
  123.4 0.7 copy.10.codes_ref
  124.1 71.2 %all-to-all-done.1 = bf16[32,24,2048]{2,1,0:T(8,128)(2,1)S(1)} async-done(((bf16[32,24,2048]{2,1,0:T(8,128)(2,1)}), bf16[32,24,2048]{2,1,0:T(8,128)(2,1)S(1)}, u32[]{:S(2)}, u32[]{:S(2)}) %all-to-all-start.1) | async-done | bytes 3145760 | tf_op jit(solution)/shard_map/all_to_all | solution.py:88
  195.3 0.0 copy-start
  195.3 1.6 copy-done
  197.0 4.3 %mix.1 = bf16[64,2048]{1,0:T(8,128)(2,1)} custom-call(bf16[768,2048]{1,0:T(8,128)(2,1)} %bitcast.23, s32[64,8]{1,0:T(8,128)} %copy.8.routes_ref, s32[64,8]{1,0:T(8,128)} %copy.10.codes_ref), custom_call_target="tpu_custom_call" | custom-call | tf_op jit(solution)/shard_map/mix/pallas_call | solution.py:91
Async XLA Ops:
  5.4 85.5 %all-to-all-start = ((bf16[32,24,2048]{2,1,0:T(8,128)(2,1)}), bf16[32,24,2048]{2,1,0:T(8,128)(2,1)S(1)}, u32[]{:S(2)}, u32[]{:S(2)}) async-start(bf16[32,24,2048]{2,1,0:T(8,128)(2,1)} %bitcast.22), calls=%async_computation | async-start | bytes 6291456 | tf_op jit(solution)/shard_map/all_to_all | solution.py:83
  18.6 76.5 %collective-permute-start = (bf16[2048,384]{1,0:T(8,128)(2,1)}, bf16[2048,384]{1,0:T(8,128)(2,1)}, u32[]{:S(2)}, u32[]{:S(2)}) collective-permute-start(bf16[2048,384]{1,0:T(8,128)(2,1)} %bitcast.30), channel_id=1, source_target_pairs={{0,1},{1,0},{2,3},{3,2},{4,5},{5,4},{6,7},{7,6},{8,9},{9,8},{10,11... | collective-permute-start | bytes 4718600 | tf_op jit(solution)/shard_map/ppermute | solution.py:67
  20.5 87.2 %collective-permute-start.1 = (bf16[2048,384]{1,0:T(8,128)(2,1)}, bf16[2048,384]{1,0:T(8,128)(2,1)}, u32[]{:S(2)}, u32[]{:S(2)}) collective-permute-start(bf16[2048,384]{1,0:T(8,128)(2,1)} %bitcast.31), channel_id=1, source_target_pairs={{0,1},{1,0},{2,3},{3,2},{4,5},{5,4},{6,7},{7,6},{8,9},{9,8},{10,11... | collective-permute-start | bytes 4718600 | tf_op jit(solution)/shard_map/ppermute | solution.py:67
  22.9 84.8 %collective-permute-start.2 = (bf16[384,2048]{1,0:T(8,128)(2,1)}, bf16[384,2048]{1,0:T(8,128)(2,1)}, u32[]{:S(2)}, u32[]{:S(2)}) collective-permute-start(bf16[384,2048]{1,0:T(8,128)(2,1)} %bitcast.32), channel_id=1, source_target_pairs={{0,1},{1,0},{2,3},{3,2},{4,5},{5,4},{6,7},{7,6},{8,9},{9,8},{10,11... | collective-permute-start | bytes 4718600 | tf_op jit(solution)/shard_map/ppermute | solution.py:67
  117.0 6.4 %copy-start.1 = (s32[64,8]{0,1:T(8,128)S(1)}, s32[64,8]{0,1:T(8,128)}, u32[]{:S(2)}) copy-start(s32[64,8]{0,1:T(8,128)} %param.10) | copy-start | bytes 6148
  117.0 78.4 %all-to-all-start.1 = ((bf16[32,24,2048]{2,1,0:T(8,128)(2,1)}), bf16[32,24,2048]{2,1,0:T(8,128)(2,1)S(1)}, u32[]{:S(2)}, u32[]{:S(2)}) async-start(bf16[32,24,2048]{2,1,0:T(8,128)(2,1)} %bitcast.28), calls=%async_computation.1 | async-start | bytes 6291456 | tf_op jit(solution)/shard_map/all_to_all | solution.py:88
  195.3 1.6 copy-start

commit v2 on v1

v2 whole, which is shorter than its diff:
```python
import jax
import jax.numpy as jnp
from jax import lax
from jax.experimental import pallas as pl
from jax.experimental.pallas import tpu as pltpu
from jax.sharding import Mesh, PartitionSpec as P

F32 = jnp.float32
BF16 = jnp.bfloat16
ROOM = 24
META = 128
VMEM = pl.BlockSpec(memory_space=pltpu.VMEM)
HBM = pl.BlockSpec(memory_space=pltpu.HBM)
NORM_LIMIT = 60
SPREAD_LIMIT = 16
EXPERT_LIMIT = 46
WEIGHTS_LIMIT = 60


def dot(a, b, dims=((1,), (0,))):
    return lax.dot_general(a, b, (dims, ((), ())), preferred_element_type=F32)


def iota(shape, dim):
    return lax.broadcasted_iota(jnp.int32, shape, dim)


def load(pairs, sems):
    copies = [pltpu.make_async_copy(a, b, sems.at[i]) for i, (a, b) in enumerate(pairs)]
    for copy in copies:
        copy.start()
    return copies


def norm_kernel(tokens_hbm, gain_hbm, routes_hbm, codes_hbm, out_ref, *scratch):
    tokens_ref, gain_ref, routes_ref, codes_ref, sems = scratch
    sources = (tokens_hbm, gain_hbm, routes_hbm, codes_hbm)
    for copy in load(zip(sources, scratch), sems):
        copy.wait()
    rows, features = tokens_ref.shape
    top = routes_ref.shape[0]
    quads = out_ref.shape[0] // rows
    near = 32 // quads
    widened = tokens_ref[...].astype(F32)
    scale = lax.rsqrt(jnp.mean(widened * widened, axis=1, keepdims=True) + 1e-06)
    normed = (widened * scale * gain_ref[...]).astype(BF16)
    codes = codes_ref[...]
    high = codes >> 6
    low = codes - (high << 6)
    one = (iota((rows, rows), 0) == iota((rows, rows), 1)).astype(BF16)
    for q in range(quads):
        listed = [routes_ref[...] - near * q, high, low]
        listed.append(jnp.zeros((META - 3 * top, rows), jnp.int32))
        listed = jnp.concatenate(listed, axis=0).astype(F32).astype(BF16)
        at = slice(q * rows, (q + 1) * rows)
        out_ref[at, :features] = normed
        out_ref[at, features:] = dot(one, listed, ((1,), (1,))).astype(BF16)


def near_keys(meta, near, rows):
    count = meta.shape[0]
    one = (iota((META, META), 0) == iota((META, META), 1)).astype(BF16)
    listed = dot(one, meta, ((1,), (1,)))
    routes, high, low = listed[0:8], listed[8:16], listed[16:24]
    names, highs, lows = [], [], []
    for e in range(near):
        same = routes == float(e)
        names.append(jnp.sum(same.astype(F32), axis=0, keepdims=True))
        highs.append(jnp.sum(jnp.where(same, high, 0.0), axis=0, keepdims=True))
        lows.append(jnp.sum(jnp.where(same, low, 0.0), axis=0, keepdims=True))
    mask = jnp.concatenate(names, axis=0)
    source, target = iota((count, count), 0), iota((count, count), 1)
    shift = rows.bit_length() - 1
    earlier = ((source < target) & (source >> shift == target >> shift)).astype(BF16)
    rank = dot(mask.astype(BF16), earlier)
    return jnp.where(mask > 0.5, rank, -1.0), highs, lows


def pair_slots(key, e, j, rows):
    line = key[e : e + 1, j * 2 * rows : (j + 1) * 2 * rows]
    slot = iota((2 * ROOM, 2 * rows), 0)
    upper = slot >= ROOM
    place = jnp.where(upper, slot - ROOM, slot).astype(F32)
    fits = upper == (iota((2 * ROOM, 2 * rows), 1) >= rows)
    return (line == place) & fits


def spread_kernel(gathered_ref, out_ref, meta_ref):
    features = out_ref.shape[1]
    count = gathered_ref.shape[0]
    near = out_ref.shape[0] // 96
    rows = 64
    meta_ref[...] = gathered_ref[:, features:]
    key, _, _ = near_keys(gathered_ref[:, features:], near, rows)
    pair = 2 * ROOM
    for j in range(count // (2 * rows)):
        chosen = [pair_slots(key, e, j, rows).astype(F32) for e in range(near)]
        chosen = jnp.concatenate(chosen, axis=0).astype(BF16)
        moved = dot(chosen, gathered_ref[j * 2 * rows : (j + 1) * 2 * rows, :features])
        for e in range(near):
            out_ref[e * 2 * pair + j * pair : e * 2 * pair + (j + 1) * pair, :] = moved[
                e * pair : (e + 1) * pair
            ].astype(BF16)


def table_kernel(meta_ref, table_ref):
    pairs, slots, _ = table_ref.shape
    near = slots // (2 * ROOM)
    rows = 64
    key, highs, lows = near_keys(meta_ref[...], near, rows)
    for j in range(pairs):
        at = slice(j * 2 * rows, (j + 1) * 2 * rows)
        for e in range(near):
            chosen = pair_slots(key, e, j, rows)
            both = [jnp.where(chosen, g[e][:, at], 0.0) for g in (highs, lows)]
            both = jnp.concatenate(both, axis=1).astype(BF16)
            table_ref[j, e * 2 * ROOM : (e + 1) * 2 * ROOM, :] = both


def gather_kernel(back_ref, table_ref, out_ref):
    pairs, slots, columns = table_ref.shape
    near = slots // (2 * ROOM)
    rows = columns // 2
    pair = 2 * ROOM
    for j in range(pairs):
        at = slice(j * rows, (j + 1) * rows)
        picked = [
            back_ref[e * 2 * pair + j * pair : e * 2 * pair + (j + 1) * pair, :]
            for e in range(near)
        ]
        total = dot(table_ref[j], jnp.concatenate(picked, axis=0), ((0,), (0,)))
        mixed = total[:rows] * (64.0 / 32768.0) + total[rows:] * (1.0 / 32768.0)
        out_ref[at, :] = mixed.astype(BF16)


def weights_kernel(*refs):
    weights, store_hbm, store, sems = refs[:6], refs[6], refs[7], refs[8]
    features, half = weights[0].shape
    pairs = []
    for i in range(2):
        for n in range(half // 128):
            at = pl.ds((i * (half // 128) + n) * features, features)
            for k in range(2):
                part = weights[3 * i + k].at[:, pl.ds(n * 128, 128)]
                pairs.append((part, store.at[at, pl.ds(k * 128, 128)]))
    base = 2 * (half // 128) * features
    for c in range(features // 256):
        for i in range(2):
            at = pl.ds(base + (2 * c + i) * half, half)
            pairs.append((weights[3 * i + 2].at[:, pl.ds(c * 256, 256)], store.at[at, :]))
    for copy in load(pairs, sems):
        copy.wait()
    copy = pltpu.make_async_copy(store, store_hbm, sems.at[0])
    copy.start()
    copy.wait()


def expert_kernel(rows_ref, weights_hbm, out_ref, store, hidden_ref, sems):
    slots, features = rows_ref.shape
    units = hidden_ref.shape[1]
    chunks = units // 128
    base = chunks * features
    steps = 2
    tile = slots // steps
    spans = [(n * features, features) for n in range(chunks)]
    spans += [(base + c * 4 * units, 4 * units) for c in range(features // 1024)]
    copies = []
    for i, (start, size) in enumerate(spans):
        at = pl.ds(start, size)
        copies.append(pltpu.make_async_copy(weights_hbm.at[at, :], store.at[at, :], sems.at[i]))
    ahead = 2
    for copy in copies[:ahead]:
        copy.start()
    for n in range(chunks):
        copies[n].wait()
        if n + ahead < len(copies):
            copies[n + ahead].start()
        for m in range(steps):
            at = slice(m * tile, (m + 1) * tile)
            both = dot(rows_ref[at, :], store[n * features : (n + 1) * features, :])
            gate, up = both[:, :128], both[:, 128:]
            value = gate / (1.0 + jnp.exp(-gate)) * up
            hidden_ref[at, n * 128 : (n + 1) * 128] = value.astype(BF16)
    for c in range(features // 256):
        if c % 4 == 0:
            copies[chunks + c // 4].wait()
        down = store[base + c * units : base + (c + 1) * units, :]
        out_ref[:, c * 256 : (c + 1) * 256] = dot(hidden_ref[...], down).astype(BF16)


def call(kernel, name, out, ins, outs=VMEM, scratch=(), limit=16):
    shapes = [jax.ShapeDtypeStruct(shape, BF16) for shape in out]
    return pl.pallas_call(
        kernel,
        out_shape=shapes if len(shapes) > 1 else shapes[0],
        in_specs=ins,
        out_specs=outs,
        scratch_shapes=scratch,
        compiler_params=pltpu.CompilerParams(vmem_limit_bytes=limit * 1024 * 1024),
        name=name,
    )


def exchanged(x, axes):
    return lax.all_to_all(x, axes, split_axis=0, concat_axis=0, tiled=True)


def local(tokens, norm_gain, routes, gate_codes, gate_weight, up_weight, down_weight):
    rows, features = tokens.shape
    top = routes.shape[1]
    quads = lax.axis_size("zh")
    near = lax.axis_size("zl") * lax.axis_size("x")
    half = gate_weight.shape[2]
    slots = quads * near * ROOM

    own = [gate_weight[0], up_weight[0], down_weight[0]]
    other = [lax.ppermute(w, "core", [(0, 1), (1, 0)]) for w in own]

    copies = call(
        norm_kernel,
        "norm",
        [(quads * rows, features + META)],
        [HBM] * 4,
        VMEM,
        [
            pltpu.VMEM((rows, features), BF16),
            pltpu.VMEM((1, features), F32),
            pltpu.VMEM((top, rows), jnp.int32),
            pltpu.VMEM((top, rows), jnp.int32),
            pltpu.SemaphoreType.DMA((4,)),
        ],
        NORM_LIMIT,
    )(tokens, norm_gain.reshape(1, features), routes.T, gate_codes.T)
    gathered = exchanged(copies, "zh")
    packed, meta = call(
        spread_kernel,
        "spread",
        [(slots, features), (quads * rows, META)],
        [VMEM],
        [VMEM, VMEM],
        limit=SPREAD_LIMIT,
    )(gathered)
    arrived = exchanged(packed, ("zl", "x"))
    table = call(table_kernel, "table", [(quads // 2, slots // 2, 4 * rows)], [VMEM])(meta)
    store = call(
        weights_kernel,
        "weights",
        [(3 * 2 * half * features // 256, 256)],
        [HBM] * 6,
        HBM,
        [
            pltpu.VMEM((3 * 2 * half * features // 256, 256), BF16),
            pltpu.SemaphoreType.DMA((4 * half // 128 + 2 * features // 256,)),
        ],
        WEIGHTS_LIMIT,
    )(*own, *other)
    arrived, table, store = lax.optimization_barrier((arrived, table, store))
    finished = call(
        expert_kernel,
        "expert",
        [(slots, features)],
        [VMEM, HBM],
        VMEM,
        [
            pltpu.VMEM(store.shape, BF16),
            pltpu.VMEM((slots, 2 * half), BF16),
            pltpu.SemaphoreType.DMA((2 * half // 128 + features // 1024,)),
        ],
        EXPERT_LIMIT,
    )(arrived, store)
    back = exchanged(finished, ("zl", "x"))
    dense = call(gather_kernel, "gather", [(quads * rows, features)], [VMEM] * 2)(back, table)
    parts = exchanged(dense, "zh").reshape(quads, rows, features)
    return jnp.sum(parts.astype(F32), axis=0).astype(BF16)


def solution(mesh):
    groups, devices = mesh.devices.shape
    wide = 4
    split = Mesh(
        mesh.devices.reshape(groups, devices // (4 * wide), 2, wide, 2),
        ("dp", "zh", "zl", "x", "core"),
    )
    tp = ("zh", "zl", "x", "core")
    placed = (
        P(("dp",) + tp, None),
        P(),
        P(("dp",) + tp, None),
        P(("dp",) + tp, None),
        P(tp, None, None),
        P(tp, None, None),
        P(tp, None, None),
    )
    return jax.shard_map(
        local, mesh=split, in_specs=placed, out_specs=P(("dp",) + tp, None), check_vma=False
    )
```

time: 202 us -> 171 us (0.85)
  waiting for transfers between devices: 137 us -> 22.1 us
  blocking collectives: 0 us -> 111 us
  matrix products: 26.1 us -> 0 us
  starting transfers between devices: 25.8 us -> 10.9 us
  Pallas kernels: 8.38 us -> 22.7 us
    all_to_all x2 -> x1, waiting for transfers between devices: 137 us -> 18.4 us  [exchanged(): return lax.all_to_all(x, axes, split_axis=0, concat_axis=0, tiled=True)]
    all_to_all x0 -> x3, blocking collectives: none -> 111 us  [exchanged(): return lax.all_to_all(x, axes, split_axis=0, concat_axis=0, tiled=True)]
    dot_general x4 -> x0, matrix products: 26.1 us -> none  [dot(): return lax.dot_general(a, b, (dims, ((), ())), preferred_element_type=F32)]
    all_to_all x2 -> x1, starting transfers between devices: 19.6 us -> 4.48 us  [exchanged(): return lax.all_to_all(x, axes, split_axis=0, concat_axis=0, tiled=True)]
    pallas_call x2 -> x6, Pallas kernels: 8.38 us -> 22.7 us  [the longest x1 10.1 us: local(): call(expert_kernel, 'expert', [(slots, features)], [VMEM, HBM], VMEM, [pl...]
    ppermute x3, waiting for transfers between devices: 0.01 us -> 3.72 us  [local(): other = [lax.ppermute(w, 'core', [(0, 1), (1, 0)]) for w in own]]
  transfers between devices with their start and end apart: 5 -> 4, of which waited for: 2 -> 3; matrix products, arithmetic and copies ran while one was open for 9% -> 0% of each run, Pallas kernels for 0% -> 5%
where the time goes in v2:
time: 171 us; the launch traced here: 170 us
  blocking collectives  111 us (65%)
  Pallas kernels  22.7 us (13%)
  waiting for transfers between devices  22.1 us (13%)
  starting transfers between devices  10.9 us (6%)
  local copies, waits for them, and re-layouts  2.28 us (1%)
    all_to_all x3, blocking collectives, exchanged(): return lax.all_to_all(x, axes, split_axis=0, concat_axis=0, tiled=True)  111 us
    all_to_all x1, waiting for transfers between devices, exchanged(): return lax.all_to_all(x, axes, split_axis=0, concat_axis=0, tiled=True)  18.4 us
    pallas_call x1, Pallas kernels, local(): call(expert_kernel, 'expert', [(slots, features)], [VMEM, HBM], VMEM, [pl...  10.1 us
    pallas_call x1, Pallas kernels, local(): call(weights_kernel, 'weights', [(3 * 2 * half * features // 256, 256)],...  7.56 us
    ppermute x3, starting transfers between devices, local(): other = [lax.ppermute(w, 'core', [(0, 1), (1, 0)]) for w in own]  6.38 us
    all_to_all x1, starting transfers between devices, exchanged(): return lax.all_to_all(x, axes, split_axis=0, concat_axis=0, tiled=True)  4.48 us
    ppermute x3, waiting for transfers between devices, local(): other = [lax.ppermute(w, 'core', [(0, 1), (1, 0)]) for w in own]  3.72 us
  transfers between devices with their start and end apart: 4, of which 3 were waited for; matrix products, arithmetic and copies ran while one was open for 0% of the time, Pallas kernels for 5%

profile of v2, /device:TPU:56, one launch (start us, length us, event | category | flops | bytes accessed | tf_op | source)
XLA Modules:
  0.0 170.5 jit_solution(2623962994039196145)
XLA Ops:
  0.0 2.2 %norm.1 = bf16[256,2176]{1,0:T(8,128)(2,1)} custom-call(bf16[64,2048]{1,0:T(8,128)(2,1)} %tokens_hbm.1, f32[1,2048]{1,0:T(1,128)} %bitcast.26, s32[8,64]{1,0:T(8,128)} %bitcast.27, s32[8,64]{1,0:T(8,128)} %bitcast.28), custom_call_target="tpu_custom_call" | custom-call | tf_op jit(solution)/shard_map/norm/pallas_call | solution.py:219
  2.2 40.3 %all_to_all.43 = bf16[4,64,2176]{2,1,0:T(8,128)(2,1)S(1)} all-to-all(bf16[4,64,2176]{2,1,0:T(8,128)(2,1)} %bitcast.19), channel_id=1, replica_groups=mesh['dp'=8,'zh'=4,'zl'=2,'x'=4,'core'=2] {'zh'}, dimensions={0} | all-to-all | bytes 2228224 | tf_op jit(solution)/shard_map/all_to_all | solution.py:205
  42.5 1.2 spread.1
  43.7 0.0 copy-start
  43.7 1.6 copy-done
  45.4 0.0 copy-start.1
  45.4 0.6 copy-done.1
  46.0 4.5 %all-to-all-start.1 = ((bf16[8,96,2048]{2,1,0:T(8,128)(2,1)}), bf16[8,96,2048]{2,1,0:T(8,128)(2,1)S(1)}, u32[]{:S(2)}, u32[]{:S(2)}) async-start(bf16[8,96,2048]{2,1,0:T(8,128)(2,1)} %bitcast.18), calls=%async_computation.1 | async-start | bytes 6291456 | tf_op jit(solution)/shard_map/all_to_all | solution.py:205
  50.5 1.9 %collective-permute-start = (bf16[2048,384]{1,0:T(8,128)(2,1)}, bf16[2048,384]{1,0:T(8,128)(2,1)}, u32[]{:S(2)}, u32[]{:S(2)}) collective-permute-start(bf16[2048,384]{1,0:T(8,128)(2,1)} %bitcast.20), channel_id=1, source_target_pairs={{0,1},{1,0},{2,3},{3,2},{4,5},{5,4},{6,7},{7,6},{8,9},{9,8},{10,11... | collective-permute-start | bytes 4718600 | tf_op jit(solution)/shard_map/ppermute | solution.py:217
  52.4 2.4 %collective-permute-start.1 = (bf16[2048,384]{1,0:T(8,128)(2,1)}, bf16[2048,384]{1,0:T(8,128)(2,1)}, u32[]{:S(2)}, u32[]{:S(2)}) collective-permute-start(bf16[2048,384]{1,0:T(8,128)(2,1)} %bitcast.22), channel_id=1, source_target_pairs={{0,1},{1,0},{2,3},{3,2},{4,5},{5,4},{6,7},{7,6},{8,9},{9,8},{10,11... | collective-permute-start | bytes 4718600 | tf_op jit(solution)/shard_map/ppermute | solution.py:217
  54.8 0.0 copy-start.2
  54.8 2.1 %collective-permute-start.2 = (bf16[384,2048]{1,0:T(8,128)(2,1)}, bf16[384,2048]{1,0:T(8,128)(2,1)}, u32[]{:S(2)}, u32[]{:S(2)}) collective-permute-start(bf16[384,2048]{1,0:T(8,128)(2,1)} %bitcast.24), channel_id=1, source_target_pairs={{0,1},{1,0},{2,3},{3,2},{4,5},{5,4},{6,7},{7,6},{8,9},{9,8},{10,11... | collective-permute-start | bytes 4718600 | tf_op jit(solution)/shard_map/ppermute | solution.py:217
  56.9 0.0 collective-permute-done.refs_3_
  56.9 1.5 collective-permute-done.1.refs_4_
  58.4 2.2 %collective-permute-done.2.refs_5_ = bf16[384,2048]{1,0:T(8,128)(2,1)} collective-permute-done((bf16[384,2048]{1,0:T(8,128)(2,1)}, bf16[384,2048]{1,0:T(8,128)(2,1)}, u32[]{:S(2)}, u32[]{:S(2)}) %collective-permute-start.2) | collective-permute-done | bytes 1572896 | tf_op jit(solution)/shard_map/ppermute | solution.py:217
  60.6 7.6 %weights.1.weights_hbm = bf16[18432,256]{1,0:T(8,128)(2,1)} custom-call(bf16[2048,384]{1,0:T(8,128)(2,1)} %bitcast.21, bf16[2048,384]{1,0:T(8,128)(2,1)} %bitcast.23, bf16[384,2048]{1,0:T(8,128)(2,1)} %bitcast.25, bf16[2048,384]{1,0:T(8,128)(2,1)} %collective-permute-done.refs_3_, bf16[2048,384]{1,0:T(8,128)(2,1)} %collective-permute-done.1.refs_4_, ...), custom_call_target="tpu_custom_call" | custom-call | tf_op jit(solution)/shard_map/weights/pallas_call | solution.py:245
  68.2 0.0 copy-done.2
  68.2 0.3 table.1.table_ref
  68.5 18.4 %all-to-all-done.1 = bf16[8,96,2048]{2,1,0:T(8,128)(2,1)S(1)} async-done(((bf16[8,96,2048]{2,1,0:T(8,128)(2,1)}), bf16[8,96,2048]{2,1,0:T(8,128)(2,1)S(1)}, u32[]{:S(2)}, u32[]{:S(2)}) %all-to-all-start.1) | async-done | bytes 3145760 | tf_op jit(solution)/shard_map/all_to_all | solution.py:205
  87.0 10.1 %expert.1 = bf16[768,2048]{1,0:T(8,128)(2,1)S(1)} custom-call(bf16[768,2048]{1,0:T(8,128)(2,1)S(1)} %bitcast.14, bf16[18432,256]{1,0:T(8,128)(2,1)} %weights.1.weights_hbm), custom_call_target="tpu_custom_call" | custom-call | tf_op jit(solution)/shard_map/expert/pallas_call | solution.py:258
  97.0 42.2 %all_to_all.44 = bf16[8,96,2048]{2,1,0:T(8,128)(2,1)S(1)} all-to-all(bf16[8,96,2048]{2,1,0:T(8,128)(2,1)S(1)} %bitcast.15), channel_id=1, replica_groups=mesh['dp'=8,'zh'=4,'zl'=2,'x'=4,'core'=2] {'zl','x'}, dimensions={0} | all-to-all | bytes 6291456 | tf_op jit(solution)/shard_map/all_to_all | solution.py:205
  139.2 1.3 gather.1
  140.5 29.0 %all_to_all.45 = bf16[4,64,2048]{2,1,0:T(8,128)(2,1)S(1)} all-to-all(bf16[4,64,2048]{2,1,0:T(8,128)(2,1)S(1)} %bitcast.17), channel_id=1, replica_groups=mesh['dp'=8,'zh'=4,'zl'=2,'x'=4,'core'=2] {'zh'}, dimensions={0} | all-to-all | bytes 2097152 | tf_op jit(solution)/shard_map/all_to_all | solution.py:205
  169.5 0.9 reduce_sum.12
Async XLA Ops:
  43.7 1.7 copy-start
  45.4 0.6 copy-start.1
  46.0 40.9 %all-to-all-start.1 = ((bf16[8,96,2048]{2,1,0:T(8,128)(2,1)}), bf16[8,96,2048]{2,1,0:T(8,128)(2,1)S(1)}, u32[]{:S(2)}, u32[]{:S(2)}) async-start(bf16[8,96,2048]{2,1,0:T(8,128)(2,1)} %bitcast.18), calls=%async_computation.1 | async-start | bytes 6291456 | tf_op jit(solution)/shard_map/all_to_all | solution.py:205
  50.5 6.4 %collective-permute-start = (bf16[2048,384]{1,0:T(8,128)(2,1)}, bf16[2048,384]{1,0:T(8,128)(2,1)}, u32[]{:S(2)}, u32[]{:S(2)}) collective-permute-start(bf16[2048,384]{1,0:T(8,128)(2,1)} %bitcast.20), channel_id=1, source_target_pairs={{0,1},{1,0},{2,3},{3,2},{4,5},{5,4},{6,7},{7,6},{8,9},{9,8},{10,11... | collective-permute-start | bytes 4718600 | tf_op jit(solution)/shard_map/ppermute | solution.py:217
  52.4 6.0 %collective-permute-start.1 = (bf16[2048,384]{1,0:T(8,128)(2,1)}, bf16[2048,384]{1,0:T(8,128)(2,1)}, u32[]{:S(2)}, u32[]{:S(2)}) collective-permute-start(bf16[2048,384]{1,0:T(8,128)(2,1)} %bitcast.22), channel_id=1, source_target_pairs={{0,1},{1,0},{2,3},{3,2},{4,5},{5,4},{6,7},{7,6},{8,9},{9,8},{10,11... | collective-permute-start | bytes 4718600 | tf_op jit(solution)/shard_map/ppermute | solution.py:217
  54.8 13.4 %copy-start.2 = (bf16[256,128]{1,0:T(8,128)(2,1)S(1)}, bf16[256,128]{1,0:T(8,128)(2,1)}, u32[]{:S(2)}) copy-start(bf16[256,128]{1,0:T(8,128)(2,1)} %copy-done.1) | copy-start | bytes 196612
  54.8 5.8 %collective-permute-start.2 = (bf16[384,2048]{1,0:T(8,128)(2,1)}, bf16[384,2048]{1,0:T(8,128)(2,1)}, u32[]{:S(2)}, u32[]{:S(2)}) collective-permute-start(bf16[384,2048]{1,0:T(8,128)(2,1)} %bitcast.24), channel_id=1, source_target_pairs={{0,1},{1,0},{2,3},{3,2},{4,5},{5,4},{6,7},{7,6},{8,9},{9,8},{10,11... | collective-permute-start | bytes 4718600 | tf_op jit(solution)/shard_map/ppermute | solution.py:217

commit v3 on v2

--- a/solution.py
+++ b/solution.py
@@ -85,36 +85,24 @@
     return (line == place) & fits
 
 
-def spread_kernel(gathered_ref, out_ref, meta_ref):
+def spread_kernel(gathered_ref, out_ref, table_ref):
     features = out_ref.shape[1]
-    count = gathered_ref.shape[0]
-    near = out_ref.shape[0] // 96
-    rows = 64
-    meta_ref[...] = gathered_ref[:, features:]
-    key, _, _ = near_keys(gathered_ref[:, features:], near, rows)
+    pairs, slots, columns = table_ref.shape
+    rows = columns // 4
     pair = 2 * ROOM
-    for j in range(count // (2 * rows)):
-        chosen = [pair_slots(key, e, j, rows).astype(F32) for e in range(near)]
-        chosen = jnp.concatenate(chosen, axis=0).astype(BF16)
-        moved = dot(chosen, gathered_ref[j * 2 * rows : (j + 1) * 2 * rows, :features])
-        for e in range(near):
-            out_ref[e * 2 * pair + j * pair : e * 2 * pair + (j + 1) * pair, :] = moved[
-                e * pair : (e + 1) * pair
-            ].astype(BF16)
-
-
-def table_kernel(meta_ref, table_ref):
-    pairs, slots, _ = table_ref.shape
-    near = slots // (2 * ROOM)
-    rows = 64
-    key, highs, lows = near_keys(meta_ref[...], near, rows)
+    near = slots // pair
+    key, highs, lows = near_keys(gathered_ref[:, features:], near, rows)
     for j in range(pairs):
         at = slice(j * 2 * rows, (j + 1) * 2 * rows)
+        chosen = [pair_slots(key, e, j, rows) for e in range(near)]
+        one = jnp.concatenate([c.astype(F32) for c in chosen], axis=0).astype(BF16)
+        moved = dot(one, gathered_ref[at, :features])
         for e in range(near):
-            chosen = pair_slots(key, e, j, rows)
-            both = [jnp.where(chosen, g[e][:, at], 0.0) for g in (highs, lows)]
+            start = e * pairs * pair + j * pair
+            out_ref[start : start + pair, :] = moved[e * pair : (e + 1) * pair].astype(BF16)
+            both = [jnp.where(chosen[e], g[e][:, at], 0.0) for g in (highs, lows)]
             both = jnp.concatenate(both, axis=1).astype(BF16)
-            table_ref[j, e * 2 * ROOM : (e + 1) * 2 * ROOM, :] = both
+            table_ref[j, e * pair : (e + 1) * pair, :] = both
 
 
 def gather_kernel(back_ref, table_ref, out_ref):
@@ -232,16 +220,6 @@
         NORM_LIMIT,
     )(tokens, norm_gain.reshape(1, features), routes.T, gate_codes.T)
     gathered = exchanged(copies, "zh")
-    packed, meta = call(
-        spread_kernel,
-        "spread",
-        [(slots, features), (quads * rows, META)],
-        [VMEM],
-        [VMEM, VMEM],
-        limit=SPREAD_LIMIT,
-    )(gathered)
-    arrived = exchanged(packed, ("zl", "x"))
-    table = call(table_kernel, "table", [(quads // 2, slots // 2, 4 * rows)], [VMEM])(meta)
     store = call(
         weights_kernel,
         "weights",
@@ -254,7 +232,16 @@
         ],
         WEIGHTS_LIMIT,
     )(*own, *other)
-    arrived, table, store = lax.optimization_barrier((arrived, table, store))
+    gathered, store = lax.optimization_barrier((gathered, store))
+    packed, table = call(
+        spread_kernel,
+        "spread",
+        [(slots, features), (quads // 2, slots // 2, 4 * rows)],
+        [VMEM],
+        [VMEM, VMEM],
+        limit=SPREAD_LIMIT,
+    )(gathered)
+    arrived = exchanged(packed, ("zl", "x"))
     finished = call(
         expert_kernel,
         "expert",

time: 171 us -> 165 us (0.965)
  waiting for transfers between devices: 22.1 us -> 4.87 us
  blocking collectives: 111 us -> 118 us
  starting transfers between devices: 10.9 us -> 16.6 us
    all_to_all x1, waiting for transfers between devices: 18.4 us -> 3.35 us  [exchanged(): return lax.all_to_all(x, axes, split_axis=0, concat_axis=0, tiled=True)]
    all_to_all x3, blocking collectives: 111 us -> 118 us  [exchanged(): return lax.all_to_all(x, axes, split_axis=0, concat_axis=0, tiled=True)]
    all_to_all x1, starting transfers between devices: 4.48 us -> 10.3 us  [exchanged(): return lax.all_to_all(x, axes, split_axis=0, concat_axis=0, tiled=True)]
    ppermute x3, waiting for transfers between devices: 3.72 us -> 1.52 us  [local(): other = [lax.ppermute(w, 'core', [(0, 1), (1, 0)]) for w in own]]
where the time goes in v3:
time: 165 us
  blocking collectives  118 us (72%)
  Pallas kernels  22.5 us (14%)
  starting transfers between devices  16.6 us (10%)
  waiting for transfers between devices  4.87 us (3%)
  local copies, waits for them, and re-layouts  2.34 us (1%)
    all_to_all x3, blocking collectives, exchanged(): return lax.all_to_all(x, axes, split_axis=0, concat_axis=0, tiled=True)  118 us
    all_to_all x1, starting transfers between devices, exchanged(): return lax.all_to_all(x, axes, split_axis=0, concat_axis=0, tiled=True)  10.3 us
    pallas_call x1, Pallas kernels, local(): call(expert_kernel, 'expert', [(slots, features)], [VMEM, HBM], VMEM, [pl...  10.1 us
    pallas_call x1, Pallas kernels, local(): call(weights_kernel, 'weights', [(3 * 2 * half * features // 256, 256)],...  7.56 us
    ppermute x3, starting transfers between devices, local(): other = [lax.ppermute(w, 'core', [(0, 1), (1, 0)]) for w in own]  6.24 us
    all_to_all x1, waiting for transfers between devices, exchanged(): return lax.all_to_all(x, axes, split_axis=0, concat_axis=0, tiled=True)  3.35 us
  transfers between devices with their start and end apart: 4, of which 3 were waited for; matrix products, arithmetic and copies ran while one was open for 0% of the time, Pallas kernels for 5%

profile of v3, /device:TPU:56, one launch (start us, length us, event | category | flops | bytes accessed | tf_op | source)
XLA Modules:
  0.0 164.9 jit_solution(4275872373767684280)
XLA Ops:
  0.0 0.0 copy-start
  0.0 2.3 %norm.1 = bf16[256,2176]{1,0:T(8,128)(2,1)} custom-call(bf16[64,2048]{1,0:T(8,128)(2,1)} %tokens_hbm.1, f32[1,2048]{1,0:T(1,128)} %bitcast.26, s32[8,64]{1,0:T(8,128)} %bitcast.27, s32[8,64]{1,0:T(8,128)} %bitcast.28), custom_call_target="tpu_custom_call" | custom-call | tf_op jit(solution)/shard_map/norm/pallas_call | solution.py:207
  2.3 10.3 %all-to-all-start = ((bf16[4,64,2176]{2,1,0:T(8,128)(2,1)}), bf16[4,64,2176]{2,1,0:T(8,128)(2,1)S(1)}, u32[]{:S(2)}, u32[]{:S(2)}) async-start(bf16[4,64,2176]{2,1,0:T(8,128)(2,1)} %bitcast.19), calls=%async_computation | async-start | bytes 2228224 | tf_op jit(solution)/shard_map/all_to_all | solution.py:193
  12.6 0.0 copy-done
  12.6 1.9 %collective-permute-start = (bf16[2048,384]{1,0:T(8,128)(2,1)S(1)}, bf16[2048,384]{1,0:T(8,128)(2,1)S(1)}, u32[]{:S(2)}, u32[]{:S(2)}) collective-permute-start(bf16[2048,384]{1,0:T(8,128)(2,1)S(1)} %bitcast.21), channel_id=1, source_target_pairs={{0,1},{1,0},{2,3},{3,2},{4,5},{5,4},{6,7},{7,6},{8,9},{9,8},{10,11... | collective-permute-start | bytes 4718600 | tf_op jit(solution)/shard_map/ppermute | solution.py:205
  14.6 2.4 %collective-permute-start.1 = (bf16[2048,384]{1,0:T(8,128)(2,1)}, bf16[2048,384]{1,0:T(8,128)(2,1)S(1)}, u32[]{:S(2)}, u32[]{:S(2)}) collective-permute-start(bf16[2048,384]{1,0:T(8,128)(2,1)} %bitcast.22), channel_id=1, source_target_pairs={{0,1},{1,0},{2,3},{3,2},{4,5},{5,4},{6,7},{7,6},{8,9},{9,8},{10,11... | collective-permute-start | bytes 4718600 | tf_op jit(solution)/shard_map/ppermute | solution.py:205
  17.0 1.9 %collective-permute-start.2 = (bf16[384,2048]{1,0:T(8,128)(2,1)}, bf16[384,2048]{1,0:T(8,128)(2,1)}, u32[]{:S(2)}, u32[]{:S(2)}) collective-permute-start(bf16[384,2048]{1,0:T(8,128)(2,1)} %bitcast.24), channel_id=1, source_target_pairs={{0,1},{1,0},{2,3},{3,2},{4,5},{5,4},{6,7},{7,6},{8,9},{9,8},{10,11... | collective-permute-start | bytes 4718600 | tf_op jit(solution)/shard_map/ppermute | solution.py:205
  18.9 0.0 collective-permute-done.refs_3_
  18.9 0.0 copy-start.1
  18.9 1.2 copy-done.1
  20.1 0.3 collective-permute-done.1.refs_4_
  20.4 0.0 copy-start.2
  20.4 1.2 copy-done.2
  21.6 1.2 collective-permute-done.2.refs_5_
  22.8 7.6 %weights.1.weights_hbm = bf16[18432,256]{1,0:T(8,128)(2,1)} custom-call(bf16[2048,384]{1,0:T(8,128)(2,1)} %bitcast.20, bf16[2048,384]{1,0:T(8,128)(2,1)} %bitcast.23, bf16[384,2048]{1,0:T(8,128)(2,1)} %bitcast.25, bf16[2048,384]{1,0:T(8,128)(2,1)} %copy-done.1, bf16[2048,384]{1,0:T(8,128)(2,1)} %copy-done.2, bf16[384,2048]{1,0:T(8,128)(2,1)} %collective-permute-done.2.refs_5_), custom_call_target="tpu_custom_call" | custom-call | tf_op jit(solution)/shard_map/weights/pallas_call | solution.py:223
  30.3 3.4 %all-to-all-done = bf16[4,64,2176]{2,1,0:T(8,128)(2,1)S(1)} async-done(((bf16[4,64,2176]{2,1,0:T(8,128)(2,1)}), bf16[4,64,2176]{2,1,0:T(8,128)(2,1)S(1)}, u32[]{:S(2)}, u32[]{:S(2)}) %all-to-all-start) | async-done | bytes 1114144 | tf_op jit(solution)/shard_map/all_to_all | solution.py:193
  33.7 1.3 spread.1
  35.0 50.6 %all_to_all.43 = bf16[8,96,2048]{2,1,0:T(8,128)(2,1)S(1)} all-to-all(bf16[8,96,2048]{2,1,0:T(8,128)(2,1)S(1)} %bitcast.18), channel_id=1, replica_groups=mesh['dp'=8,'zh'=4,'zl'=2,'x'=4,'core'=2] {'zl','x'}, dimensions={0} | all-to-all | bytes 6291456 | tf_op jit(solution)/shard_map/all_to_all | solution.py:193
  85.5 10.1 %expert.1 = bf16[768,2048]{1,0:T(8,128)(2,1)S(1)} custom-call(bf16[768,2048]{1,0:T(8,128)(2,1)S(1)} %bitcast.14, bf16[18432,256]{1,0:T(8,128)(2,1)} %weights.1.weights_hbm), custom_call_target="tpu_custom_call" | custom-call | tf_op jit(solution)/shard_map/expert/pallas_call | solution.py:245
  95.6 39.9 %all_to_all.44 = bf16[8,96,2048]{2,1,0:T(8,128)(2,1)S(1)} all-to-all(bf16[8,96,2048]{2,1,0:T(8,128)(2,1)S(1)} %bitcast.15), channel_id=1, replica_groups=mesh['dp'=8,'zh'=4,'zl'=2,'x'=4,'core'=2] {'zl','x'}, dimensions={0} | all-to-all | bytes 6291456 | tf_op jit(solution)/shard_map/all_to_all | solution.py:193
  135.5 1.3 gather.1
  136.8 27.2 %all_to_all.45 = bf16[4,64,2048]{2,1,0:T(8,128)(2,1)S(1)} all-to-all(bf16[4,64,2048]{2,1,0:T(8,128)(2,1)S(1)} %bitcast.17), channel_id=1, replica_groups=mesh['dp'=8,'zh'=4,'zl'=2,'x'=4,'core'=2] {'zh'}, dimensions={0} | all-to-all | bytes 2097152 | tf_op jit(solution)/shard_map/all_to_all | solution.py:193
  164.0 0.9 reduce_sum.12
Async XLA Ops:
  0.0 12.6 %copy-start = (bf16[1,2048,384]{2,1,0:T(8,128)(2,1)S(1)}, bf16[1,2048,384]{2,1,0:T(8,128)(2,1)}, u32[]{:S(2)}) copy-start(bf16[1,2048,384]{2,1,0:T(8,128)(2,1)} %param.11) | copy-start | bytes 4718596
  2.3 31.4 %all-to-all-start = ((bf16[4,64,2176]{2,1,0:T(8,128)(2,1)}), bf16[4,64,2176]{2,1,0:T(8,128)(2,1)S(1)}, u32[]{:S(2)}, u32[]{:S(2)}) async-start(bf16[4,64,2176]{2,1,0:T(8,128)(2,1)} %bitcast.19), calls=%async_computation | async-start | bytes 2228224 | tf_op jit(solution)/shard_map/all_to_all | solution.py:193
  12.6 6.3 %collective-permute-start = (bf16[2048,384]{1,0:T(8,128)(2,1)S(1)}, bf16[2048,384]{1,0:T(8,128)(2,1)S(1)}, u32[]{:S(2)}, u32[]{:S(2)}) collective-permute-start(bf16[2048,384]{1,0:T(8,128)(2,1)S(1)} %bitcast.21), channel_id=1, source_target_pairs={{0,1},{1,0},{2,3},{3,2},{4,5},{5,4},{6,7},{7,6},{8,9},{9,8},{10,11... | collective-permute-start | bytes 4718600 | tf_op jit(solution)/shard_map/ppermute | solution.py:205
  14.6 5.8 %collective-permute-start.1 = (bf16[2048,384]{1,0:T(8,128)(2,1)}, bf16[2048,384]{1,0:T(8,128)(2,1)S(1)}, u32[]{:S(2)}, u32[]{:S(2)}) collective-permute-start(bf16[2048,384]{1,0:T(8,128)(2,1)} %bitcast.22), channel_id=1, source_target_pairs={{0,1},{1,0},{2,3},{3,2},{4,5},{5,4},{6,7},{7,6},{8,9},{9,8},{10,11... | collective-permute-start | bytes 4718600 | tf_op jit(solution)/shard_map/ppermute | solution.py:205
  17.0 5.8 %collective-permute-start.2 = (bf16[384,2048]{1,0:T(8,128)(2,1)}, bf16[384,2048]{1,0:T(8,128)(2,1)}, u32[]{:S(2)}, u32[]{:S(2)}) collective-permute-start(bf16[384,2048]{1,0:T(8,128)(2,1)} %bitcast.24), channel_id=1, source_target_pairs={{0,1},{1,0},{2,3},{3,2},{4,5},{5,4},{6,7},{7,6},{8,9},{9,8},{10,11... | collective-permute-start | bytes 4718600 | tf_op jit(solution)/shard_map/ppermute | solution.py:205
  18.9 1.2 copy-start.1
  20.4 1.2 copy-start.2

commit v4 on v3

--- a/solution.py
+++ b/solution.py
@@ -8,13 +8,15 @@
 F32 = jnp.float32
 BF16 = jnp.bfloat16
 ROOM = 24
-META = 128
+LANES = 128
+META = 16
 VMEM = pl.BlockSpec(memory_space=pltpu.VMEM)
 HBM = pl.BlockSpec(memory_space=pltpu.HBM)
 NORM_LIMIT = 60
 SPREAD_LIMIT = 16
 EXPERT_LIMIT = 46
 WEIGHTS_LIMIT = 60
+STEPS = 4
 
 
 def dot(a, b, dims=((1,), (0,))):
@@ -39,7 +41,8 @@
         copy.wait()
     rows, features = tokens_ref.shape
     top = routes_ref.shape[0]
-    quads = out_ref.shape[0] // rows
+    size = rows * features // LANES + META
+    quads = out_ref.shape[0] // size
     near = 32 // quads
     widened = tokens_ref[...].astype(F32)
     scale = lax.rsqrt(jnp.mean(widened * widened, axis=1, keepdims=True) + 1e-06)
@@ -47,21 +50,23 @@
     codes = codes_ref[...]
     high = codes >> 6
     low = codes - (high << 6)
-    one = (iota((rows, rows), 0) == iota((rows, rows), 1)).astype(BF16)
+    blank = jnp.zeros((META - top, LANES - rows), jnp.int32)
     for q in range(quads):
-        listed = [routes_ref[...] - near * q, high, low]
-        listed.append(jnp.zeros((META - 3 * top, rows), jnp.int32))
-        listed = jnp.concatenate(listed, axis=0).astype(F32).astype(BF16)
-        at = slice(q * rows, (q + 1) * rows)
-        out_ref[at, :features] = normed
-        out_ref[at, features:] = dot(one, listed, ((1,), (1,))).astype(BF16)
-
-
-def near_keys(meta, near, rows):
-    count = meta.shape[0]
-    one = (iota((META, META), 0) == iota((META, META), 1)).astype(BF16)
-    listed = dot(one, meta, ((1,), (1,)))
-    routes, high, low = listed[0:8], listed[8:16], listed[16:24]
+        for c in range(features // LANES):
+            at = slice(q * size + c * rows, q * size + (c + 1) * rows)
+            out_ref[at, :] = normed[:, c * LANES : (c + 1) * LANES]
+        upper = jnp.concatenate([routes_ref[...] - near * q, high], axis=1)
+        lower = jnp.concatenate([low, blank], axis=1)
+        listed = jnp.concatenate([upper, lower], axis=0).astype(F32).astype(BF16)
+        out_ref[q * size + size - META : (q + 1) * size, :] = listed
+
+
+def near_keys(metas, near, rows):
+    count = len(metas) * rows
+    half = META // 2
+    routes = jnp.concatenate([m[:half, :rows] for m in metas], axis=1)
+    high = jnp.concatenate([m[:half, rows:] for m in metas], axis=1)
+    low = jnp.concatenate([m[half:, :rows] for m in metas], axis=1)
     names, highs, lows = [], [], []
     for e in range(near):
         same = routes == float(e)
@@ -91,15 +96,30 @@
     rows = columns // 4
     pair = 2 * ROOM
     near = slots // pair
-    key, highs, lows = near_keys(gathered_ref[:, features:], near, rows)
+    size = rows * features // LANES + META
+    metas = [
+        gathered_ref[(q + 1) * size - META : (q + 1) * size, :].astype(F32)
+        for q in range(2 * pairs)
+    ]
+    key, highs, lows = near_keys(metas, near, rows)
     for j in range(pairs):
         at = slice(j * 2 * rows, (j + 1) * 2 * rows)
         chosen = [pair_slots(key, e, j, rows) for e in range(near)]
         one = jnp.concatenate([c.astype(F32) for c in chosen], axis=0).astype(BF16)
-        moved = dot(one, gathered_ref[at, :features])
+        for c in range(features // (2 * LANES)):
+            block = []
+            for q in (2 * j, 2 * j + 1):
+                start = q * size + 2 * c * rows
+                left = gathered_ref[start : start + rows, :]
+                right = gathered_ref[start + rows : start + 2 * rows, :]
+                block.append(jnp.concatenate([left, right], axis=1))
+            moved = dot(one, jnp.concatenate(block, axis=0)).astype(BF16)
+            for e in range(near):
+                start = e * pairs * pair + j * pair
+                out_ref[start : start + pair, 2 * c * LANES : 2 * (c + 1) * LANES] = moved[
+                    e * pair : (e + 1) * pair
+                ]
         for e in range(near):
-            start = e * pairs * pair + j * pair
-            out_ref[start : start + pair, :] = moved[e * pair : (e + 1) * pair].astype(BF16)
             both = [jnp.where(chosen[e], g[e][:, at], 0.0) for g in (highs, lows)]
             both = jnp.concatenate(both, axis=1).astype(BF16)
             table_ref[j, e * pair : (e + 1) * pair, :] = both
@@ -124,18 +144,20 @@
 def weights_kernel(*refs):
     weights, store_hbm, store, sems = refs[:6], refs[6], refs[7], refs[8]
     features, half = weights[0].shape
+    more = half - 128
     pairs = []
     for i in range(2):
-        for n in range(half // 128):
-            at = pl.ds((i * (half // 128) + n) * features, features)
-            for k in range(2):
-                part = weights[3 * i + k].at[:, pl.ds(n * 128, 128)]
-                pairs.append((part, store.at[at, pl.ds(k * 128, 128)]))
-    base = 2 * (half // 128) * features
+        at = pl.ds(i * features, features)
+        for k in range(2):
+            part = weights[3 * i + k]
+            pairs.append((part.at[:, pl.ds(0, 128)], store.at[at, pl.ds(k * 128, 128)]))
+            pairs.append((part.at[:, pl.ds(128, more)], store.at[at, pl.ds(256 + k * more, more)]))
+    band = 2 * half // 256
     for c in range(features // 256):
         for i in range(2):
-            at = pl.ds(base + (2 * c + i) * half, half)
-            pairs.append((weights[3 * i + 2].at[:, pl.ds(c * 256, 256)], store.at[at, :]))
+            at = pl.ds(2 * features + (2 * (c // band) + i) * half, half)
+            to = store.at[at, pl.ds(c % band * 256, 256)]
+            pairs.append((weights[3 * i + 2].at[:, pl.ds(c * 256, 256)], to))
     for copy in load(pairs, sems):
         copy.wait()
     copy = pltpu.make_async_copy(store, store_hbm, sems.at[0])
@@ -146,34 +168,50 @@
 def expert_kernel(rows_ref, weights_hbm, out_ref, store, hidden_ref, sems):
     slots, features = rows_ref.shape
     units = hidden_ref.shape[1]
-    chunks = units // 128
-    base = chunks * features
-    steps = 2
-    tile = slots // steps
-    spans = [(n * features, features) for n in range(chunks)]
-    spans += [(base + c * 4 * units, 4 * units) for c in range(features // 1024)]
-    copies = []
-    for i, (start, size) in enumerate(spans):
-        at = pl.ds(start, size)
-        copies.append(pltpu.make_async_copy(weights_hbm.at[at, :], store.at[at, :], sems.at[i]))
-    ahead = 2
-    for copy in copies[:ahead]:
-        copy.start()
-    for n in range(chunks):
-        copies[n].wait()
-        if n + ahead < len(copies):
-            copies[n + ahead].start()
+    half = units // 2
+    more = half - 128
+    band = units // 256
+
+    def piece(i, start, size, lo, width):
+        at = (pl.ds(start, size), pl.ds(lo, width))
+        return pltpu.make_async_copy(weights_hbm.at[at], store.at[at], sems.at[i])
+
+    copies = [
+        piece(0, 0, features, 0, 256),
+        piece(1, 0, features, 256, 2 * more),
+        piece(2, features, features, 0, units),
+        piece(3, 2 * features, store.shape[0] - 2 * features, 0, units),
+    ]
+    copies[0].start()
+    copies[1].start()
+
+    def product(start, lo, width, steps, parts):
+        tile = slots // steps
         for m in range(steps):
             at = slice(m * tile, (m + 1) * tile)
-            both = dot(rows_ref[at, :], store[n * features : (n + 1) * features, :])
-            gate, up = both[:, :128], both[:, 128:]
-            value = gate / (1.0 + jnp.exp(-gate)) * up
-            hidden_ref[at, n * 128 : (n + 1) * 128] = value.astype(BF16)
+            both = dot(rows_ref[at, :], store[start : start + features, lo : lo + width])
+            for gate_lo, up_lo, size, to in parts:
+                gate, up = both[:, gate_lo : gate_lo + size], both[:, up_lo : up_lo + size]
+                value = gate / (1.0 + jnp.exp(-gate)) * up
+                hidden_ref[at, to : to + size] = value.astype(BF16)
+
+    copies[0].wait()
+    copies[2].start()
+    product(0, 0, 256, 2, [(0, 128, 128, 0)])
+    copies[1].wait()
+    copies[3].start()
+    product(0, 256, 2 * more, STEPS, [(0, more, more, 128)])
+    copies[2].wait()
+    product(
+        features, 0, units, STEPS, [(0, 128, 128, half), (256, 256 + more, more, half + 128)]
+    )
+    copies[3].wait()
     for c in range(features // 256):
-        if c % 4 == 0:
-            copies[chunks + c // 4].wait()
-        down = store[base + c * units : base + (c + 1) * units, :]
-        out_ref[:, c * 256 : (c + 1) * 256] = dot(hidden_ref[...], down).astype(BF16)
+        start = 2 * features + c // band * units
+        down = store[start : start + units, c % band * 256 : (c % band + 1) * 256]
+        for m in range(2):
+            at = slice(m * slots // 2, (m + 1) * slots // 2)
+            out_ref[at, c * 256 : (c + 1) * 256] = dot(hidden_ref[at, :], down).astype(BF16)
 
 
 def call(kernel, name, out, ins, outs=VMEM, scratch=(), limit=16):
@@ -207,7 +245,7 @@
     copies = call(
         norm_kernel,
         "norm",
-        [(quads * rows, features + META)],
+        [(quads * (rows * features // LANES + META), LANES)],
         [HBM] * 4,
         VMEM,
         [
@@ -220,15 +258,16 @@
         NORM_LIMIT,
     )(tokens, norm_gain.reshape(1, features), routes.T, gate_codes.T)
     gathered = exchanged(copies, "zh")
+    bands = -(-features // (2 * half))
     store = call(
         weights_kernel,
         "weights",
-        [(3 * 2 * half * features // 256, 256)],
+        [(2 * features + bands * 2 * half, 2 * half)],
         [HBM] * 6,
         HBM,
         [
-            pltpu.VMEM((3 * 2 * half * features // 256, 256), BF16),
-            pltpu.SemaphoreType.DMA((4 * half // 128 + 2 * features // 256,)),
+            pltpu.VMEM((2 * features + bands * 2 * half, 2 * half), BF16),
+            pltpu.SemaphoreType.DMA((8 + 2 * features // 256,)),
         ],
         WEIGHTS_LIMIT,
     )(*own, *other)
@@ -251,7 +290,7 @@
         [
             pltpu.VMEM(store.shape, BF16),
             pltpu.VMEM((slots, 2 * half), BF16),
-            pltpu.SemaphoreType.DMA((2 * half // 128 + features // 1024,)),
+            pltpu.SemaphoreType.DMA((4,)),
         ],
         EXPERT_LIMIT,
     )(arrived, store)

time: 165 us -> 163 us (0.988)
  no operation moved by 1% of the time
where the time goes in v4:
time: 163 us
  blocking collectives  117 us (72%)
  Pallas kernels  21.8 us (13%)
  starting transfers between devices  16.6 us (10%)
  waiting for transfers between devices  4.16 us (3%)
  local copies, waits for them, and re-layouts  2.34 us (1%)
    all_to_all x3, blocking collectives, exchanged(): return lax.all_to_all(x, axes, split_axis=0, concat_axis=0, tiled=True)  117 us
    all_to_all x1, starting transfers between devices, exchanged(): return lax.all_to_all(x, axes, split_axis=0, concat_axis=0, tiled=True)  10.3 us
    pallas_call x1, Pallas kernels, local(): call(expert_kernel, 'expert', [(slots, features)], [VMEM, HBM], VMEM, [pl...  9.32 us
    pallas_call x1, Pallas kernels, local(): call(weights_kernel, 'weights', [(2 * features + bands * 2 * half, 2 * ha...  7.67 us
    ppermute x3, starting transfers between devices, local(): other = [lax.ppermute(w, 'core', [(0, 1), (1, 0)]) for w in own]  6.24 us
  transfers between devices with their start and end apart: 4, of which 3 were waited for; matrix products, arithmetic and copies ran while one was open for 0% of the time, Pallas kernels for 5%

profile of v4, /device:TPU:56, one launch (start us, length us, event | category | flops | bytes accessed | tf_op | source)
XLA Modules:
  0.0 162.9 jit_solution(14861088139119281355)
XLA Ops:
  0.0 0.0 copy-start
  0.0 2.3 %norm.1 = bf16[4160,128]{1,0:T(8,128)(2,1)} custom-call(bf16[64,2048]{1,0:T(8,128)(2,1)} %tokens_hbm.1, f32[1,2048]{1,0:T(1,128)} %bitcast.26, s32[8,64]{1,0:T(8,128)} %bitcast.27, s32[8,64]{1,0:T(8,128)} %bitcast.28), custom_call_target="tpu_custom_call" | custom-call | tf_op jit(solution)/shard_map/norm/pallas_call | solution.py:245
  2.3 10.3 %all-to-all-start = ((bf16[4,1040,128]{2,1,0:T(8,128)(2,1)}), bf16[4,1040,128]{2,1,0:T(8,128)(2,1)S(1)}, u32[]{:S(2)}, u32[]{:S(2)}) async-start(bf16[4,1040,128]{2,1,0:T(8,128)(2,1)} %bitcast.19), calls=%async_computation | async-start | bytes 2129920 | tf_op jit(solution)/shard_map/all_to_all | solution.py:231
  12.6 0.0 copy-done
  12.6 1.9 %collective-permute-start = (bf16[2048,384]{1,0:T(8,128)(2,1)S(1)}, bf16[2048,384]{1,0:T(8,128)(2,1)S(1)}, u32[]{:S(2)}, u32[]{:S(2)}) collective-permute-start(bf16[2048,384]{1,0:T(8,128)(2,1)S(1)} %bitcast.21), channel_id=1, source_target_pairs={{0,1},{1,0},{2,3},{3,2},{4,5},{5,4},{6,7},{7,6},{8,9},{9,8},{10,11... | collective-permute-start | bytes 4718600 | tf_op jit(solution)/shard_map/ppermute | solution.py:243
  14.5 2.4 %collective-permute-start.1 = (bf16[2048,384]{1,0:T(8,128)(2,1)}, bf16[2048,384]{1,0:T(8,128)(2,1)S(1)}, u32[]{:S(2)}, u32[]{:S(2)}) collective-permute-start(bf16[2048,384]{1,0:T(8,128)(2,1)} %bitcast.22), channel_id=1, source_target_pairs={{0,1},{1,0},{2,3},{3,2},{4,5},{5,4},{6,7},{7,6},{8,9},{9,8},{10,11... | collective-permute-start | bytes 4718600 | tf_op jit(solution)/shard_map/ppermute | solution.py:243
  16.9 1.9 %collective-permute-start.2 = (bf16[384,2048]{1,0:T(8,128)(2,1)}, bf16[384,2048]{1,0:T(8,128)(2,1)}, u32[]{:S(2)}, u32[]{:S(2)}) collective-permute-start(bf16[384,2048]{1,0:T(8,128)(2,1)} %bitcast.24), channel_id=1, source_target_pairs={{0,1},{1,0},{2,3},{3,2},{4,5},{5,4},{6,7},{7,6},{8,9},{9,8},{10,11... | collective-permute-start | bytes 4718600 | tf_op jit(solution)/shard_map/ppermute | solution.py:243
  18.9 0.0 collective-permute-done.refs_3_
  18.9 0.0 copy-start.1
  18.9 1.1 copy-done.1
  20.0 0.3 collective-permute-done.1.refs_4_
  20.4 0.0 copy-start.2
  20.4 1.2 copy-done.2
  21.5 1.2 collective-permute-done.2.refs_5_
  22.7 7.7 %weights.1.weights_hbm = bf16[6400,768]{1,0:T(8,128)(2,1)} custom-call(bf16[2048,384]{1,0:T(8,128)(2,1)} %bitcast.20, bf16[2048,384]{1,0:T(8,128)(2,1)} %bitcast.23, bf16[384,2048]{1,0:T(8,128)(2,1)} %bitcast.25, bf16[2048,384]{1,0:T(8,128)(2,1)} %copy-done.1, bf16[2048,384]{1,0:T(8,128)(2,1)} %copy-done.2, bf16[384,2048]{1,0:T(8,128)(2,1)} %collective-permute-done.2.refs_5_), custom_call_target="tpu_custom_call" | custom-call | tf_op jit(solution)/shard_map/weights/pallas_call | solution.py:262
  30.4 2.6 %all-to-all-done = bf16[4,1040,128]{2,1,0:T(8,128)(2,1)S(1)} async-done(((bf16[4,1040,128]{2,1,0:T(8,128)(2,1)}), bf16[4,1040,128]{2,1,0:T(8,128)(2,1)S(1)}, u32[]{:S(2)}, u32[]{:S(2)}) %all-to-all-start) | async-done | bytes 1064992 | tf_op jit(solution)/shard_map/all_to_all | solution.py:231
  33.1 1.2 spread.1
  34.3 50.1 %all_to_all.43 = bf16[8,96,2048]{2,1,0:T(8,128)(2,1)S(1)} all-to-all(bf16[8,96,2048]{2,1,0:T(8,128)(2,1)S(1)} %bitcast.18), channel_id=1, replica_groups=mesh['dp'=8,'zh'=4,'zl'=2,'x'=4,'core'=2] {'zl','x'}, dimensions={0} | all-to-all | bytes 6291456 | tf_op jit(solution)/shard_map/all_to_all | solution.py:231
  84.4 9.3 %expert.1 = bf16[768,2048]{1,0:T(8,128)(2,1)S(1)} custom-call(bf16[768,2048]{1,0:T(8,128)(2,1)S(1)} %bitcast.14, bf16[6400,768]{1,0:T(8,128)(2,1)} %weights.1.weights_hbm), custom_call_target="tpu_custom_call" | custom-call | tf_op jit(solution)/shard_map/expert/pallas_call | solution.py:284
  93.7 39.9 %all_to_all.44 = bf16[8,96,2048]{2,1,0:T(8,128)(2,1)S(1)} all-to-all(bf16[8,96,2048]{2,1,0:T(8,128)(2,1)S(1)} %bitcast.15), channel_id=1, replica_groups=mesh['dp'=8,'zh'=4,'zl'=2,'x'=4,'core'=2] {'zl','x'}, dimensions={0} | all-to-all | bytes 6291456 | tf_op jit(solution)/shard_map/all_to_all | solution.py:231
  133.6 1.3 gather.1
  134.9 27.1 %all_to_all.45 = bf16[4,64,2048]{2,1,0:T(8,128)(2,1)S(1)} all-to-all(bf16[4,64,2048]{2,1,0:T(8,128)(2,1)S(1)} %bitcast.17), channel_id=1, replica_groups=mesh['dp'=8,'zh'=4,'zl'=2,'x'=4,'core'=2] {'zh'}, dimensions={0} | all-to-all | bytes 2097152 | tf_op jit(solution)/shard_map/all_to_all | solution.py:231
  162.0 0.9 reduce_sum.12
Async XLA Ops:
  0.0 12.6 %copy-start = (bf16[1,2048,384]{2,1,0:T(8,128)(2,1)S(1)}, bf16[1,2048,384]{2,1,0:T(8,128)(2,1)}, u32[]{:S(2)}) copy-start(bf16[1,2048,384]{2,1,0:T(8,128)(2,1)} %param.11) | copy-start | bytes 4718596
  2.3 30.8 %all-to-all-start = ((bf16[4,1040,128]{2,1,0:T(8,128)(2,1)}), bf16[4,1040,128]{2,1,0:T(8,128)(2,1)S(1)}, u32[]{:S(2)}, u32[]{:S(2)}) async-start(bf16[4,1040,128]{2,1,0:T(8,128)(2,1)} %bitcast.19), calls=%async_computation | async-start | bytes 2129920 | tf_op jit(solution)/shard_map/all_to_all | solution.py:231
  12.6 6.3 %collective-permute-start = (bf16[2048,384]{1,0:T(8,128)(2,1)S(1)}, bf16[2048,384]{1,0:T(8,128)(2,1)S(1)}, u32[]{:S(2)}, u32[]{:S(2)}) collective-permute-start(bf16[2048,384]{1,0:T(8,128)(2,1)S(1)} %bitcast.21), channel_id=1, source_target_pairs={{0,1},{1,0},{2,3},{3,2},{4,5},{5,4},{6,7},{7,6},{8,9},{9,8},{10,11... | collective-permute-start | bytes 4718600 | tf_op jit(solution)/shard_map/ppermute | solution.py:243
  14.5 5.8 %collective-permute-start.1 = (bf16[2048,384]{1,0:T(8,128)(2,1)}, bf16[2048,384]{1,0:T(8,128)(2,1)S(1)}, u32[]{:S(2)}, u32[]{:S(2)}) collective-permute-start(bf16[2048,384]{1,0:T(8,128)(2,1)} %bitcast.22), channel_id=1, source_target_pairs={{0,1},{1,0},{2,3},{3,2},{4,5},{5,4},{6,7},{7,6},{8,9},{9,8},{10,11... | collective-permute-start | bytes 4718600 | tf_op jit(solution)/shard_map/ppermute | solution.py:243
  16.9 5.8 %collective-permute-start.2 = (bf16[384,2048]{1,0:T(8,128)(2,1)}, bf16[384,2048]{1,0:T(8,128)(2,1)}, u32[]{:S(2)}, u32[]{:S(2)}) collective-permute-start(bf16[384,2048]{1,0:T(8,128)(2,1)} %bitcast.24), channel_id=1, source_target_pairs={{0,1},{1,0},{2,3},{3,2},{4,5},{5,4},{6,7},{7,6},{8,9},{9,8},{10,11... | collective-permute-start | bytes 4718600 | tf_op jit(solution)/shard_map/ppermute | solution.py:243
  18.9 1.2 copy-start.1
  20.4 1.2 copy-start.2

commit v5 on v4

--- a/solution.py
+++ b/solution.py
@@ -141,6 +141,14 @@
         out_ref[at, :] = mixed.astype(BF16)
 
 
+def sum_kernel(parts_ref, out_ref):
+    rows = out_ref.shape[0]
+    total = parts_ref[:rows, :].astype(F32)
+    for q in range(1, parts_ref.shape[0] // rows):
+        total = total + parts_ref[q * rows : (q + 1) * rows, :].astype(F32)
+    out_ref[...] = total.astype(BF16)
+
+
 def weights_kernel(*refs):
     weights, store_hbm, store, sems = refs[:6], refs[6], refs[7], refs[8]
     features, half = weights[0].shape
@@ -197,7 +205,7 @@
 
     copies[0].wait()
     copies[2].start()
-    product(0, 0, 256, 2, [(0, 128, 128, 0)])
+    product(0, 0, 256, 4, [(0, 128, 128, 0)])
     copies[1].wait()
     copies[3].start()
     product(0, 256, 2 * more, STEPS, [(0, more, more, 128)])
@@ -296,8 +304,8 @@
     )(arrived, store)
     back = exchanged(finished, ("zl", "x"))
     dense = call(gather_kernel, "gather", [(quads * rows, features)], [VMEM] * 2)(back, table)
-    parts = exchanged(dense, "zh").reshape(quads, rows, features)
-    return jnp.sum(parts.astype(F32), axis=0).astype(BF16)
+    parts = exchanged(dense, "zh")
+    return call(sum_kernel, "sum", [(rows, features)], [VMEM])(parts)
 
 
 def solution(mesh):

time: 163 us -> 163 us (level)
  no operation moved by 1% of the time
where the time goes in v5:
time: 163 us
  blocking collectives  117 us (72%)
  Pallas kernels  22.6 us (14%)
  starting transfers between devices  16.6 us (10%)
  waiting for transfers between devices  4.13 us (3%)
  local copies, waits for them, and re-layouts  2.36 us (1%)
    all_to_all x3, blocking collectives, exchanged(): return lax.all_to_all(x, axes, split_axis=0, concat_axis=0, tiled=True)  117 us
    all_to_all x1, starting transfers between devices, exchanged(): return lax.all_to_all(x, axes, split_axis=0, concat_axis=0, tiled=True)  10.3 us
    pallas_call x1, Pallas kernels, local(): call(expert_kernel, 'expert', [(slots, features)], [VMEM, HBM], VMEM, [pl...  9.34 us
    pallas_call x1, Pallas kernels, local(): call(weights_kernel, 'weights', [(2 * features + bands * 2 * half, 2 * ha...  7.68 us
    ppermute x3, starting transfers between devices, local(): other = [lax.ppermute(w, 'core', [(0, 1), (1, 0)]) for w in own]  6.24 us
  transfers between devices with their start and end apart: 4, of which 3 were waited for; matrix products, arithmetic and copies ran while one was open for 0% of the time, Pallas kernels for 5%

profile of v5, /device:TPU:56, one launch (start us, length us, event | category | flops | bytes accessed | tf_op | source)
XLA Modules:
  0.0 162.8 jit_solution(8600660063850568937)
XLA Ops:
  0.0 0.0 copy-start
  0.0 2.3 %norm.1 = bf16[4160,128]{1,0:T(8,128)(2,1)} custom-call(bf16[64,2048]{1,0:T(8,128)(2,1)} %tokens_hbm.1, f32[1,2048]{1,0:T(1,128)} %bitcast.28, s32[8,64]{1,0:T(8,128)} %bitcast.29, s32[8,64]{1,0:T(8,128)} %bitcast.30), custom_call_target="tpu_custom_call" | custom-call | tf_op jit(solution)/shard_map/norm/pallas_call | solution.py:253
  2.3 10.3 %all-to-all-start = ((bf16[4,1040,128]{2,1,0:T(8,128)(2,1)}), bf16[4,1040,128]{2,1,0:T(8,128)(2,1)S(1)}, u32[]{:S(2)}, u32[]{:S(2)}) async-start(bf16[4,1040,128]{2,1,0:T(8,128)(2,1)} %bitcast.21), calls=%async_computation | async-start | bytes 2129920 | tf_op jit(solution)/shard_map/all_to_all | solution.py:239
  12.6 0.0 copy-done
  12.6 1.9 %collective-permute-start = (bf16[2048,384]{1,0:T(8,128)(2,1)S(1)}, bf16[2048,384]{1,0:T(8,128)(2,1)S(1)}, u32[]{:S(2)}, u32[]{:S(2)}) collective-permute-start(bf16[2048,384]{1,0:T(8,128)(2,1)S(1)} %bitcast.23), channel_id=1, source_target_pairs={{0,1},{1,0},{2,3},{3,2},{4,5},{5,4},{6,7},{7,6},{8,9},{9,8},{10,11... | collective-permute-start | bytes 4718600 | tf_op jit(solution)/shard_map/ppermute | solution.py:251
  14.5 2.4 %collective-permute-start.1 = (bf16[2048,384]{1,0:T(8,128)(2,1)}, bf16[2048,384]{1,0:T(8,128)(2,1)S(1)}, u32[]{:S(2)}, u32[]{:S(2)}) collective-permute-start(bf16[2048,384]{1,0:T(8,128)(2,1)} %bitcast.24), channel_id=1, source_target_pairs={{0,1},{1,0},{2,3},{3,2},{4,5},{5,4},{6,7},{7,6},{8,9},{9,8},{10,11... | collective-permute-start | bytes 4718600 | tf_op jit(solution)/shard_map/ppermute | solution.py:251
  16.9 1.9 %collective-permute-start.2 = (bf16[384,2048]{1,0:T(8,128)(2,1)}, bf16[384,2048]{1,0:T(8,128)(2,1)}, u32[]{:S(2)}, u32[]{:S(2)}) collective-permute-start(bf16[384,2048]{1,0:T(8,128)(2,1)} %bitcast.26), channel_id=1, source_target_pairs={{0,1},{1,0},{2,3},{3,2},{4,5},{5,4},{6,7},{7,6},{8,9},{9,8},{10,11... | collective-permute-start | bytes 4718600 | tf_op jit(solution)/shard_map/ppermute | solution.py:251
  18.9 0.0 collective-permute-done.refs_3_
  18.9 0.0 copy-start.1
  18.9 1.2 copy-done.1
  20.1 0.3 collective-permute-done.1.refs_4_
  20.4 0.0 copy-start.2
  20.4 1.2 copy-done.2
  21.6 1.2 collective-permute-done.2.refs_5_
  22.7 7.7 %weights.1.weights_hbm = bf16[6400,768]{1,0:T(8,128)(2,1)} custom-call(bf16[2048,384]{1,0:T(8,128)(2,1)} %bitcast.22, bf16[2048,384]{1,0:T(8,128)(2,1)} %bitcast.25, bf16[384,2048]{1,0:T(8,128)(2,1)} %bitcast.27, bf16[2048,384]{1,0:T(8,128)(2,1)} %copy-done.1, bf16[2048,384]{1,0:T(8,128)(2,1)} %copy-done.2, bf16[384,2048]{1,0:T(8,128)(2,1)} %collective-permute-done.2.refs_5_), custom_call_target="tpu_custom_call" | custom-call | tf_op jit(solution)/shard_map/weights/pallas_call | solution.py:270
  30.4 2.6 %all-to-all-done = bf16[4,1040,128]{2,1,0:T(8,128)(2,1)S(1)} async-done(((bf16[4,1040,128]{2,1,0:T(8,128)(2,1)}), bf16[4,1040,128]{2,1,0:T(8,128)(2,1)S(1)}, u32[]{:S(2)}, u32[]{:S(2)}) %all-to-all-start) | async-done | bytes 1064992 | tf_op jit(solution)/shard_map/all_to_all | solution.py:239
  33.1 1.2 spread.1
  34.3 50.1 %all_to_all.45 = bf16[8,96,2048]{2,1,0:T(8,128)(2,1)S(1)} all-to-all(bf16[8,96,2048]{2,1,0:T(8,128)(2,1)S(1)} %bitcast.20), channel_id=1, replica_groups=mesh['dp'=8,'zh'=4,'zl'=2,'x'=4,'core'=2] {'zl','x'}, dimensions={0} | all-to-all | bytes 6291456 | tf_op jit(solution)/shard_map/all_to_all | solution.py:239
  84.4 9.3 %expert.1 = bf16[768,2048]{1,0:T(8,128)(2,1)S(1)} custom-call(bf16[768,2048]{1,0:T(8,128)(2,1)S(1)} %bitcast.15, bf16[6400,768]{1,0:T(8,128)(2,1)} %weights.1.weights_hbm), custom_call_target="tpu_custom_call" | custom-call | tf_op jit(solution)/shard_map/expert/pallas_call | solution.py:292
  93.8 39.9 %all_to_all.46 = bf16[8,96,2048]{2,1,0:T(8,128)(2,1)S(1)} all-to-all(bf16[8,96,2048]{2,1,0:T(8,128)(2,1)S(1)} %bitcast.16), channel_id=1, replica_groups=mesh['dp'=8,'zh'=4,'zl'=2,'x'=4,'core'=2] {'zl','x'}, dimensions={0} | all-to-all | bytes 6291456 | tf_op jit(solution)/shard_map/all_to_all | solution.py:239
  133.6 1.3 gather.1
  134.9 27.1 %all_to_all.47 = bf16[4,64,2048]{2,1,0:T(8,128)(2,1)S(1)} all-to-all(bf16[4,64,2048]{2,1,0:T(8,128)(2,1)S(1)} %bitcast.19), channel_id=1, replica_groups=mesh['dp'=8,'zh'=4,'zl'=2,'x'=4,'core'=2] {'zh'}, dimensions={0} | all-to-all | bytes 2097152 | tf_op jit(solution)/shard_map/all_to_all | solution.py:239
  162.0 0.8 sum.1
Async XLA Ops:
  0.0 12.6 %copy-start = (bf16[1,2048,384]{2,1,0:T(8,128)(2,1)S(1)}, bf16[1,2048,384]{2,1,0:T(8,128)(2,1)}, u32[]{:S(2)}) copy-start(bf16[1,2048,384]{2,1,0:T(8,128)(2,1)} %param.11) | copy-start | bytes 4718596
  2.3 30.8 %all-to-all-start = ((bf16[4,1040,128]{2,1,0:T(8,128)(2,1)}), bf16[4,1040,128]{2,1,0:T(8,128)(2,1)S(1)}, u32[]{:S(2)}, u32[]{:S(2)}) async-start(bf16[4,1040,128]{2,1,0:T(8,128)(2,1)} %bitcast.21), calls=%async_computation | async-start | bytes 2129920 | tf_op jit(solution)/shard_map/all_to_all | solution.py:239
  12.6 6.3 %collective-permute-start = (bf16[2048,384]{1,0:T(8,128)(2,1)S(1)}, bf16[2048,384]{1,0:T(8,128)(2,1)S(1)}, u32[]{:S(2)}, u32[]{:S(2)}) collective-permute-start(bf16[2048,384]{1,0:T(8,128)(2,1)S(1)} %bitcast.23), channel_id=1, source_target_pairs={{0,1},{1,0},{2,3},{3,2},{4,5},{5,4},{6,7},{7,6},{8,9},{9,8},{10,11... | collective-permute-start | bytes 4718600 | tf_op jit(solution)/shard_map/ppermute | solution.py:251
  14.5 5.8 %collective-permute-start.1 = (bf16[2048,384]{1,0:T(8,128)(2,1)}, bf16[2048,384]{1,0:T(8,128)(2,1)S(1)}, u32[]{:S(2)}, u32[]{:S(2)}) collective-permute-start(bf16[2048,384]{1,0:T(8,128)(2,1)} %bitcast.24), channel_id=1, source_target_pairs={{0,1},{1,0},{2,3},{3,2},{4,5},{5,4},{6,7},{7,6},{8,9},{9,8},{10,11... | collective-permute-start | bytes 4718600 | tf_op jit(solution)/shard_map/ppermute | solution.py:251
  16.9 5.8 %collective-permute-start.2 = (bf16[384,2048]{1,0:T(8,128)(2,1)}, bf16[384,2048]{1,0:T(8,128)(2,1)}, u32[]{:S(2)}, u32[]{:S(2)}) collective-permute-start(bf16[384,2048]{1,0:T(8,128)(2,1)} %bitcast.26), channel_id=1, source_target_pairs={{0,1},{1,0},{2,3},{3,2},{4,5},{5,4},{6,7},{7,6},{8,9},{9,8},{10,11... | collective-permute-start | bytes 4718600 | tf_op jit(solution)/shard_map/ppermute | solution.py:251
  18.9 1.2 copy-start.1
  20.4 1.2 copy-start.2
